TPU v7x, 512 devices: a whole 4x4x16 slice. The times are simulated.
512 devices in a mesh: tile: 8 (over x, core), mask: 2 (over z_hi), pencil: 32 (over y, z_lo).
Axes of the slice: x: 4, y: 4, z: 16 (z_hi: 2, z_lo: 8; z = z_hi * 8 + z_lo), core: 2. Of those that a mesh axis runs over, the one named last changes fastest.
Arguments:
- mask_field: float32 [8, 2, 4096, 4096], P('tile', 'mask', 'pencil'), may hold values from 0 to 1
- design_target: bfloat16 [8, 4096, 4096], P('tile', 'pencil'), may hold values from 0 to 1
- kernel_spectra: float32 [2, 4, 256, 256], P(None, None, 'pencil'), may hold values from -32 to 32
- support_radii: int32 [4], replicated, may hold values from 64 to 128
- edge_points: int32 [8, 3, 8192], P('tile', None, 'pencil'), may hold values from 0 to 4095, as said below
- point_weights: float32 [8, 8192], P('tile', 'pencil'), may hold values from 1 to 27
Outputs:
- updated_mask: bfloat16 [8, 2, 4096, 4096], P('tile', 'mask', 'pencil')
- total_loss: float32 [], replicated
Inputs may be any that keep to these rules, and one draw needn't show every extreme that they name: edge_points[t, 0, i] is a row and edge_points[t, 1, i] a column of tile t; for i in the j-th aligned block of 256 points the row lies in j * 128 + 1 to j * 128 + 126, and every block reaches both ends; columns lie in 1 to 4094; edge_points[t, 2, i] is the normal code 0 to 3.
All inputs are finite; a program needn't handle non-finite values.
Results may differ from a plain program's by a relative error of at most 0.013.
Values may be sent and summed in bfloat16 or wider, within the bound.
A program may use at most 128 MiB of HBM per device.

v0:
```python
import math

import jax
import jax.numpy as jnp
from jax import lax
from jax.sharding import PartitionSpec as P

N = 4096
SPLIT = 64
INNER = 64
BANDS = 4
KEEP = 256


STEEPNESS = 6.0
THRESHOLD = 0.5
STEP_SIZE = 0.2
EPSILON = 1e-06


def partner_2(block, axis, stride):
    count = lax.axis_size(axis)
    route = []
    for low in range(count):
        high = low | 1 << stride
        if high != low and high < count:
            route += [(low, high), (high, low)]
    return lax.ppermute(block, axis, route)


def phase_pair(phase_index, period, direction):
    angle = 2.0 * math.pi / period * phase_index.astype(jnp.float32)
    return (jnp.cos(angle), direction * jnp.sin(angle))


def complex_table(phase_index, period, direction):
    cosine_table, sine_table = phase_pair(phase_index, period, direction)
    upper = jnp.stack([cosine_table, sine_table], axis=1)
    lower = jnp.stack([-sine_table, cosine_table], axis=1)
    return jnp.stack([upper, lower], axis=0).astype(jnp.bfloat16)


def joint_table(phase_index, direction):
    cosine_table, sine_table = phase_pair(phase_index, N, direction)
    upper = jnp.stack([cosine_table, sine_table])
    lower = jnp.stack([-sine_table, cosine_table])
    return jnp.stack([upper, lower]).astype(jnp.bfloat16)


def build_tables():
    inner_range = jnp.arange(INNER, dtype=jnp.int32)
    outer_range = jnp.arange(SPLIT, dtype=jnp.int32)
    band_range = jnp.arange(BANDS, dtype=jnp.int32) - BANDS // 2
    square_index = jnp.mod(inner_range[:, None] * inner_range[None, :], INNER)
    cross_index = jnp.mod(outer_range[:, None] * band_range[None, :], SPLIT)
    first_index = jnp.mod(
        inner_range[None, :, None] * inner_range[None, None, :] * SPLIT
        + outer_range[:, None, None] * inner_range[None, None, :],
        N,
    )
    back_index = jnp.mod(
        band_range[None, :, None] * outer_range[None, None, :] * INNER
        + inner_range[:, None, None] * outer_range[None, None, :],
        N,
    )
    ahead_first = joint_table(first_index, -1.0)
    ahead_last = complex_table(cross_index, SPLIT, -1.0)
    back_first = joint_table(back_index, 1.0)
    back_last = complex_table(square_index, INNER, 1.0)
    return (ahead_first, ahead_last, back_first, back_last)


def contract(form, left, right):
    return jnp.einsum(form, left, right, preferred_element_type=jnp.float32)


def forward_pass(values, tables, transposed):
    ahead_first, ahead_last, back_first, back_last = tables
    pieces, groups, batch_rows = (values.shape[0], values.shape[1], values.shape[2])
    split_form = values.reshape(pieces, groups, batch_rows, INNER, SPLIT)
    turned = contract("pgmba,pqabk->qgmak", split_form, ahead_first[:pieces]).astype(jnp.bfloat16)
    if transposed:
        return contract("pgmak,paqj->qgjkm", turned, ahead_last).reshape(
            2, groups, KEEP, batch_rows
        )
    return contract("pgmak,paqj->qgmjk", turned, ahead_last).reshape(2, groups, batch_rows, KEEP)


def inverse_pass(band_data, tables, transposed, pieces):
    ahead_first, ahead_last, back_first, back_last = tables
    groups = band_data.shape[1]
    if transposed:
        batch_rows = band_data.shape[3]
        split_form = band_data.reshape(2, groups, BANDS, INNER, batch_rows)
        turned = contract("pgjkm,pqkja->qgmak", split_form, back_first)
    else:
        batch_rows = band_data.shape[2]
        split_form = band_data.reshape(2, groups, batch_rows, BANDS, INNER)
        turned = contract("pgmjk,pqkja->qgmak", split_form, back_first)
    turned = turned.astype(jnp.bfloat16)
    result = contract("pgmak,pkqb->qgmba", turned, back_last[:, :, :pieces])
    return result.reshape(pieces, groups, batch_rows, N)


def product_band(spectra, spectrum, factor):
    kernel_real, kernel_imag = (spectra[0], spectra[1])
    mask_real, mask_imag = (spectrum[0], spectrum[1])
    return jnp.stack(
        [
            (kernel_real * mask_real - kernel_imag * mask_imag) * factor,
            (kernel_real * mask_imag + kernel_imag * mask_real) * factor,
        ]
    ).astype(jnp.bfloat16)


def adjoint_band(spectra, backs, factor):
    kernel_real, kernel_imag = (spectra[0], spectra[1])
    back_real, back_imag = (backs[0], backs[1])
    summed_real = jnp.sum(kernel_real * back_real + kernel_imag * back_imag, axis=0) * factor
    summed_imag = jnp.sum(kernel_real * back_imag - kernel_imag * back_real, axis=0) * factor
    return jnp.stack([summed_real, summed_imag])[:, None].astype(jnp.bfloat16)


def per_device(
    mask_field, design_target, kernel_spectra, support_radii, edge_points, point_weights
):
    tables = build_tables()
    local_rows = mask_field.shape[2]
    kept_local = kernel_spectra.shape[2]
    pencil = lax.axis_index("pencil")
    freq_cols = pencil * kept_local + jnp.arange(kept_local, dtype=jnp.int32) - KEEP // 2
    freq_rows = jnp.arange(KEEP, dtype=jnp.int32) - KEEP // 2
    radius_sq = freq_cols[:, None] ** 2 + freq_rows[None, :] ** 2
    inside = (radius_sq[None] <= (support_radii**2)[:, None, None]).astype(jnp.float32)
    spectra = kernel_spectra * inside[None]
    image = mask_field.astype(jnp.bfloat16)
    lined = forward_pass(image, tables, True).astype(jnp.bfloat16)
    columns = lax.all_to_all(lined, "pencil", split_axis=2, concat_axis=3, tiled=True)
    spectrum = forward_pass(columns, tables, False)
    band_data = product_band(spectra, spectrum, 1.0 / (N * N))
    partial_value = inverse_pass(band_data, tables, False, 2).astype(jnp.bfloat16)
    fields = inverse_pass(
        lax.all_to_all(partial_value, "pencil", split_axis=3, concat_axis=2, tiled=True),
        tables,
        True,
        2,
    ).astype(jnp.bfloat16)
    intensity = jnp.sum(jnp.square(fields.astype(jnp.float32)), axis=(0, 1))
    resist = jax.nn.sigmoid(STEEPNESS * (intensity - THRESHOLD)).astype(jnp.bfloat16)
    goals = jnp.array([0.5, 1.0, 0.0], dtype=jnp.float32)[:, None]
    weights = point_weights[0]
    point_row = edge_points[0, 0] - pencil * local_rows
    point_col = edge_points[0, 1]
    normal = edge_points[0, 2]
    step_row = (normal == 0).astype(jnp.int32) - (normal == 1).astype(jnp.int32)
    step_col = (normal == 2).astype(jnp.int32) - (normal == 3).astype(jnp.int32)
    places = jnp.stack(
        [
            point_row * N + point_col,
            (point_row - step_row) * N + (point_col - step_col),
            (point_row + step_row) * N + (point_col + step_col),
        ]
    )
    target_rows = design_target[0]
    partner = partner_2(resist, "mask", 0)
    own_resist = resist.astype(jnp.float32)
    other_resist = partner.astype(jnp.float32)
    union = own_resist + other_resist - own_resist * other_resist
    gap = union - target_rows.astype(jnp.float32)
    at_points = union.reshape(-1)[places]
    missed = at_points - goals
    local_loss = 0.5 * (jnp.sum(gap * gap) + jnp.sum(weights[None] * missed * missed))
    pushes = 2.0 * weights[None] * missed
    scattered = (
        jnp.zeros((local_rows * N,), jnp.float32).at[places.reshape(-1)].add(pushes.reshape(-1))
    )
    grad_union = 2.0 * gap + scattered.reshape(local_rows, N)
    drive = (
        grad_union * (1.0 - other_resist) * STEEPNESS * own_resist * (1.0 - own_resist)
    ).astype(jnp.bfloat16)
    loss_total = lax.psum(local_loss, ("tile", "mask", "pencil"))
    mixed = (drive.astype(jnp.float32)[None, None] * fields.astype(jnp.float32)).astype(
        jnp.bfloat16
    )
    adjoint_lines = forward_pass(mixed, tables, True).astype(jnp.bfloat16)
    backs = forward_pass(
        lax.all_to_all(adjoint_lines, "pencil", split_axis=2, concat_axis=3, tiled=True),
        tables,
        False,
    )
    band_grad = adjoint_band(spectra, backs, 2.0 / (N * N))
    grad_partial = inverse_pass(band_grad, tables, False, 2).astype(jnp.bfloat16)
    grad_lines = lax.all_to_all(grad_partial, "pencil", split_axis=3, concat_axis=2, tiled=True)
    gradient = inverse_pass(grad_lines, tables, True, 1)[0, 0]
    squares = jnp.sum(gradient * gradient)
    square_total = lax.psum(squares, ("tile", "mask", "pencil"))
    tile_total = lax.axis_size("tile")
    mask_total = lax.axis_size("mask")
    spread = jnp.sqrt(square_total / (tile_total * mask_total * N * N) + EPSILON)
    updated = (mask_field[0, 0] - STEP_SIZE * gradient / spread).astype(jnp.bfloat16)
    return (updated.reshape(1, 1, local_rows, N), loss_total / (tile_total * N * N))


def solution(mesh):
    placed = (
        P("tile", "mask", "pencil", None),
        P("tile", "pencil", None),
        P(None, None, "pencil", None),
        P(),
        P("tile", None, "pencil"),
        P("tile", "pencil"),
    )
    return jax.shard_map(
        per_device,
        mesh=mesh,
        in_specs=placed,
        out_specs=(P("tile", "mask", "pencil", None), P()),
        check_vma=False,
    )
```

profile of v0, /device:TPU:1, one launch (start us, length us, event | category | flops | bytes accessed | tf_op | source)
XLA Modules:
  0.0 518.7 jit_solution(2187577742039484677)
XLA Ops:
  0.9 1.9 copy.251
  2.9 9.2 %negate_convert_fusion = (bf16[1,64,64,64]{2,3,0,1:T(8,128)(2,1)S(1)}, bf16[1,64,64,64]{2,3,0,1:T(8,128)(2,1)S(1)}, bf16[1,64,64,64]{2,3,0,1:T(8,128)(2,1)S(1)}) fusion(s32[64,64]{1,0:T(8,128)S(1)} %iota_multiply_fusion, s32[64,64]{0,1:T(8,128)S(1)} %copy.210), kind=kLoop, calls=%fused_computation.65 | loop fusion | flops 4980736 | bytes 1605632 | tf_op jit(solution)/shard_map/convert.14
  12.1 1.4 convert_bitcast_fusion
  13.6 1.3 fusion.67
  15.7 16.4 %all-to-all-start = ((bf16[2,1,256,128]{3,0,1,2:T(2,128)(2,1)}), bf16[2,1,256,128]{3,0,1,2:T(2,128)(2,1)}, u32[]{:S(2)}, u32[]{:S(2)}) async-start(bf16[2,1,256,128]{3,0,1,2:T(2,128)(2,1)} %copy.215), calls=%async_computation | async-start | bytes 262144 | tf_op jit(solution)/shard_map/all_to_all | solution.py:138
  32.5 4.6 fusion.50
  40.1 3.7 all-to-all-done
  45.1 3.9 fusion.20
  51.6 1.9 fusion.42
  53.5 1.9 copy.222
  55.5 1.9 fusion.43
  57.4 9.4 %copy.292 = bf16[2,4,8,64,64]{2,1,0,4,3:T(4,128)(2,1)} copy(bf16[2,4,8,64,64]{4,3,2,1,0:T(8,128)(2,1)S(1)} %fusion.43) | data formatting | bytes 1048576 | tf_op jit(solution)/shard_map/convert_element_type | solution.py:141
  66.8 10.5 %reshape.1116 = bf16[32,2,4096]{2,1,0:T(2,128)(2,1)S(1)} reshape(bf16[4096,2,4,8]{3,2,1,0:T(4,128)(2,1)} %bitcast.366) | data formatting | bytes 1048576
  77.3 37.7 %all_to_all.60 = bf16[32,2,4096]{2,1,0:T(2,128)(2,1)S(1)} all-to-all(bf16[32,2,4096]{2,1,0:T(2,128)(2,1)S(1)} %reshape.1116), channel_id=1, replica_groups=mesh['tile'=8,'mask'=2,'pencil'=32] {'pencil'}, dimensions={0} | all-to-all | bytes 1048576 | tf_op jit(solution)/shard_map/all_to_all | solution.py:143
  114.9 10.9 %reshape.1117 = bf16[4096,2,4,8]{3,2,1,0:T(4,128)(2,1)} reshape(bf16[32,2,4096]{2,1,0:T(2,128)(2,1)S(1)} %all_to_all.60) | data formatting | bytes 1048576
  125.8 10.2 %copy.294 = bf16[2,4,8,32,128]{4,2,3,1,0:T(8,128)(2,1)S(1)} copy(bf16[2,4,8,32,128]{2,1,0,4,3:T(4,128)(2,1)} %bitcast.367) | data formatting | bytes 1048576 | tf_op jit(solution)/shard_map/all_to_all | solution.py:143
  136.1 5.9 %fusion.12 = bf16[2,4,128,64,64]{2,3,1,0,4:T(8,128)(2,1)} fusion(bf16[2,4,4,64,128,1]{4,3,2,1,0,5:T(8,128)(2,1)S(1)} %bitcast.375, bf16[1,2,64,4,64]{4,3,0,1,2:T(4,128)(2,1)S(1)} %get-tuple-element.27, bf16[1,2,64,4,64]{4,3,0,1,2:T(4,128)(2,1)S(1)} %get-tuple-element.26), kind=kOutput, calls=%fused_computation.17 | convolution fusion | flops 71565312 | bytes 9043968 | tf_op jit(solution)/shard_map/pgjkm,pqkja->qgmak/dot_general | solution.py:74
  142.0 18.2 %fusion = (f32[128,64,64]{0,1,2:T(8,128)S(1)}, bf16[2,64,4,128,64]{3,1,4,2,0:T(8,128)(2,1)}) fusion(bf16[2,4,128,64,64]{2,3,1,0,4:T(8,128)(2,1)} %fusion.12, bf16[1,64,2,64]{1,3,0,2:T(8,128)(2,1)S(1)} %get-tuple-element.37, bf16[1,64,2,64]{1,3,0,2:T(8,128)(2,1)S(1)} %get-tuple-element.36), kind=kOutput, calls=%fused_computation.5 | convolution fusion | flops 1090060288 | bytes 18907136 | tf_op jit(solution)/shard_map/pgmak,pkqb->qgmba/dot_general | solution.py:74
  161.4 8.0 %collective-permute-start = (bf16[128,4096]{0,1:T(8,128)(2,1)S(1)}, bf16[128,4096]{0,1:T(8,128)(2,1)}, u32[]{:S(2)}, u32[]{:S(2)}) collective-permute-start(bf16[128,4096]{0,1:T(8,128)(2,1)S(1)} %bitcast.369), channel_id=1, source_target_pairs={{0,32},{32,0},{1,33},{33,1},{2,34},{34,2},{3,35},{35,3},{4,36},{36... | collective-permute-start | bytes 3145736 | tf_op jit(solution)/shard_map/ppermute | solution.py:28
  171.4 2.3 copy.229
  173.6 1.3 fusion.116
  176.2 82.6 %collective-permute-done = bf16[128,4096]{0,1:T(8,128)(2,1)} collective-permute-done((bf16[128,4096]{0,1:T(8,128)(2,1)S(1)}, bf16[128,4096]{0,1:T(8,128)(2,1)}, u32[]{:S(2)}, u32[]{:S(2)}) %collective-permute-start) | collective-permute-done | bytes 1048608 | tf_op jit(solution)/shard_map/ppermute | solution.py:28
  258.7 2.9 fusion.25
  261.6 2.9 copy.230
  264.5 3.3 copy.307
  267.8 8.9 %gather_fusion = f32[768]{0:T(1024)S(1)} fusion(f32[524288]{0:T(1024)} %bitcast.368, s32[1024]{0:T(1024)S(1)} %pad_clamp_fusion), kind=kCustom, calls=%fused_computation | custom fusion | bytes 9216 | tf_op jit(solution)/shard_map/gather | solution.py:170
  276.7 1.4 fusion.111
  278.0 6.6 %scatter_custom_fusion = f32[524288]{0:T(1024)} fusion(s32[768]{0:T(1024)} %fusion.116, f32[768]{0:T(1024)S(1)} %reshape.1069, f32[]{:T(128)} %constant.54.clone.1), kind=kCustom, calls=%fused_computation.92 | custom fusion | flops 768 | bytes 2097664 | tf_op jit(solution)/shard_map/scatter-add | solution.py:175
  284.7 2.7 reshape.1033
  287.4 2.9 copy.231
  290.3 4.1 multiply_reduce_fusion
  294.5 1.9 copy.232
  296.4 11.6 %fusion.13 = bf16[2,4,128,64,64]{2,4,1,0,3:T(8,128)(2,1)} fusion(bf16[2,64,4,128,64]{3,1,4,2,0:T(8,128)(2,1)} %get-tuple-element.49, f32[128,64,64]{0,1,2:T(8,128)} %copy.232, bf16[1,2,64,64,64]{3,4,1,2,0:T(8,128)(2,1)} %get-tuple-element.21, bf16[1,2,64,64,64]{3,4,1,2,0:T(8,128)(2,1)} %get-tuple-element.20), kind=kOutput, calls=%fused_computation.18 | convolution fusion | flops 1091567616 | bytes 20971520 | tf_op jit(solution)/shard_map/pgmba,pqabk->qgmak/dot_general | solution.py:74
  308.0 8.0 %fusion.54 = bf16[2,4,4,64,128]{4,2,3,1,0:T(4,128)(2,1)S(1)} fusion(bf16[2,4,128,64,64]{2,4,1,0,3:T(8,128)(2,1)} %fusion.13, bf16[1,64,2,4]{1,3,0,2:T(4,128)(2,1)S(1)} %copy-done.5, bf16[1,64,2,4]{1,3,0,2:T(4,128)(2,1)S(1)} %copy-done.3), kind=kOutput, calls=%fused_computation.76 | convolution fusion | flops 67375104 | bytes 8914944 | tf_op jit(solution)/shard_map/pgmak,paqj->qgjkm/dot_general | solution.py:74
  316.5 39.2 %all_to_all.61 = bf16[2,4,256,128]{3,1,0,2:T(4,128)(2,1)S(1)} all-to-all(bf16[2,4,256,128]{3,1,0,2:T(4,128)(2,1)S(1)} %copy.237), channel_id=1, replica_groups=mesh['tile'=8,'mask'=2,'pencil'=32] {'pencil'}, dimensions={2} | all-to-all | bytes 1048576 | tf_op jit(solution)/shard_map/all_to_all | solution.py:187
  356.8 1.6 reshape.1034
  358.5 2.3 copy.274
  360.8 4.5 fusion.44
  367.7 3.8 copy.301
  371.5 7.2 %reshape.1118 = bf16[32,2,1024]{2,1,0:T(2,128)(2,1)} reshape(bf16[4096,1,2,8]{3,2,1,0:T(2,128)(2,1)} %bitcast.371) | data formatting | bytes 262144
  378.7 5.4 %all-to-all-start.3 = ((bf16[32,2,1024]{2,1,0:T(2,128)(2,1)}), bf16[32,2,1024]{2,1,0:T(2,128)(2,1)S(1)}, u32[]{:S(2)}, u32[]{:S(2)}) async-start(bf16[32,2,1024]{2,1,0:T(2,128)(2,1)} %reshape.1118), calls=%async_computation.3 | async-start | bytes 262144 | tf_op jit(solution)/shard_map/all_to_all | solution.py:193
  385.5 10.5 %all-to-all-done.3 = bf16[32,2,1024]{2,1,0:T(2,128)(2,1)S(1)} async-done(((bf16[32,2,1024]{2,1,0:T(2,128)(2,1)}), bf16[32,2,1024]{2,1,0:T(2,128)(2,1)S(1)}, u32[]{:S(2)}, u32[]{:S(2)}) %all-to-all-start.3) | async-done | bytes 131104 | tf_op jit(solution)/shard_map/all_to_all | solution.py:193
  395.9 3.5 reshape.1119
  399.4 4.5 copy.303
  404.8 3.4 fusion.32
  408.2 103.1 %all-reduce = (f32[]{:T(128)}, f32[]{:T(128)}) all-reduce(f32[]{:T(128)} %get-tuple-element.50, f32[]{:T(128)S(6)} %mul.732), channel_id=1, replica_groups=mesh['tile'=8,'mask'=2,'pencil'=32] {'tile','mask','pencil'}, use_global_device_ids=true, to_apply=%region_5.6 | all-reduce | flops 2 | bytes 16 | tf_op jit(solution)/shard_map/psum | solution.py:196
  512.0 1.8 fusion.31
  515.4 1.3 copy.252
  (85 shorter events, 19.2 us)
Async XLA Ops:
  12.1 1.5 copy-start
  12.1 1.5 copy-start.1
  12.1 1.5 copy-start.2
  12.1 1.5 copy-start.4
  15.7 28.1 %all-to-all-start = ((bf16[2,1,256,128]{3,0,1,2:T(2,128)(2,1)}), bf16[2,1,256,128]{3,0,1,2:T(2,128)(2,1)}, u32[]{:S(2)}, u32[]{:S(2)}) async-start(bf16[2,1,256,128]{3,0,1,2:T(2,128)(2,1)} %copy.215), calls=%async_computation | async-start | bytes 262144 | tf_op jit(solution)/shard_map/all_to_all | solution.py:138
  45.1 4.0 copy-start.3
  45.1 4.0 copy-start.5
  160.2 9.2 %copy-start.9 = (s32[1,3,256]{2,0,1:T(1,128)S(1)}, s32[1,3,256]{2,0,1:T(1,128)}, u32[]{:S(2)}) copy-start(s32[1,3,256]{2,0,1:T(1,128)} %param.11) | copy-start | bytes 9220
  161.4 97.3 %collective-permute-start = (bf16[128,4096]{0,1:T(8,128)(2,1)S(1)}, bf16[128,4096]{0,1:T(8,128)(2,1)}, u32[]{:S(2)}, u32[]{:S(2)}) collective-permute-start(bf16[128,4096]{0,1:T(8,128)(2,1)S(1)} %bitcast.369), channel_id=1, source_target_pairs={{0,32},{32,0},{1,33},{33,1},{2,34},{34,2},{3,35},{35,3},{4,36},{36... | collective-permute-start | bytes 3145736 | tf_op jit(solution)/shard_map/ppermute | solution.py:28
  169.4 0.6 copy-start.6
  169.4 0.6 copy-start.7
  169.5 0.6 copy-start.8
  378.7 17.2 %all-to-all-start.3 = ((bf16[32,2,1024]{2,1,0:T(2,128)(2,1)}), bf16[32,2,1024]{2,1,0:T(2,128)(2,1)S(1)}, u32[]{:S(2)}, u32[]{:S(2)}) async-start(bf16[32,2,1024]{2,1,0:T(2,128)(2,1)} %reshape.1118), calls=%async_computation.3 | async-start | bytes 262144 | tf_op jit(solution)/shard_map/all_to_all | solution.py:193
where the time goes:
time: 524 us; the launch traced here: 519 us
  blocking collectives  180 us (34%)
  local copies, waits for them, and re-layouts  104 us (20%)
  waiting for transfers between devices  96.7 us (18%)
  matrix products  64.6 us (12%)
  other arithmetic  38.5 us (7%)
  starting transfers between devices  29.8 us (6%)
    psum x1, blocking collectives, per_device(): square_total = lax.psum(squares, ('tile', 'mask', 'pencil'))  103 us
    ppermute x1, waiting for transfers between devices, partner_2(): return lax.ppermute(block, axis, route)  82.6 us
    dot_general x16, matrix products, contract(): return jnp.einsum(form, left, right, preferred_element_type=jnp.float32)  64.6 us
    unnamed x29, local copies, waits for them, and re-layouts  42.1 us
    all_to_all x1, blocking collectives, per_device(): lax.all_to_all(adjoint_lines, 'pencil', split_axis=2, concat_axis=3, tile...  39.2 us
    all_to_all x1, blocking collectives, per_device(): lax.all_to_all(partial_value, 'pencil', split_axis=3, concat_axis=2, tile...  37.7 us
    all_to_all x1, starting transfers between devices, per_device(): lax.all_to_all(lined, 'pencil', split_axis=2, concat_axis=3, tiled=True)  16.4 us
    another operation x8, other arithmetic  10.7 us
  transfers between devices with their start and end apart: 3, of which 3 were waited for; matrix products, arithmetic and copies ran while one was open for 3% of the time, Pallas kernels for 0%

commit v1 on v0

v1 whole, which is shorter than its diff:
```python
import functools
import math

import jax
import jax.numpy as jnp
import numpy as np
from jax import lax
from jax.experimental import pallas as pl
from jax.experimental.pallas import tpu as pltpu
from jax.sharding import PartitionSpec as P
from ml_dtypes import bfloat16

N = 4096
KEEP = 256
HALF = 128
KERN = 4
ROWS = 128
SAMPLES = 512
PENCIL = 32
CHUNK = 512
PTS = 256
FIRST = 2
EPSILON = 1e-06
STEP_SIZE = 0.2
F32 = jnp.float32
BF16 = jnp.bfloat16
MESH = pl.DeviceIdType.MESH
VMEM = pltpu.VMEM
DMA = pltpu.SemaphoreType.DMA


def angles(first, second, period):
    return 2.0 * np.pi / period * ((first[:, None] * second[None, :]) % period)


@functools.cache
def tables():
    pixels = np.arange(N)
    freqs = np.arange(KEEP) - HALF
    half = np.arange(136)
    theta = angles(half, pixels, N)
    theta_cos, theta_sin = (np.cos(theta), np.sin(theta))
    theta_cos[129:], theta_sin[129:] = (0.0, 0.0)
    ahead = np.stack([theta_cos.reshape(17, 8, N), -theta_sin.reshape(17, 8, N)], axis=1).reshape(272, N)
    theta = angles(pixels, freqs, N)
    ahead_x = np.concatenate([np.cos(theta), np.sin(theta)], axis=1)
    theta_cos, theta_sin = (np.cos(theta), np.sin(theta))
    back_x = np.concatenate(
        [
            np.concatenate([theta_cos, -theta_sin], axis=1).reshape(PENCIL, ROWS, 512),
            np.concatenate([theta_sin, theta_cos], axis=1).reshape(PENCIL, ROWS, 512),
        ],
        axis=1,
    )
    theta = angles(np.abs(freqs), np.arange(SAMPLES), SAMPLES)
    sign = np.where(freqs < 0, -1.0, 1.0)[:, None]
    back_y = np.concatenate(
        [
            np.concatenate([np.cos(theta), sign * np.sin(theta)], axis=1),
            np.concatenate([-np.sin(theta), sign * np.cos(theta)], axis=1),
        ],
        axis=0,
    )
    shift = np.arange(N)
    bell = np.ones(N)
    for freq in range(1, 256):
        bell += 2.0 * np.cos(2.0 * np.pi / N * ((freq * shift) % N))
    bell /= SAMPLES
    bell += np.cos(2.0 * np.pi / N * ((256 * shift) % N)) / SAMPLES
    spread = bell[(pixels[None, :] - 8 * np.arange(SAMPLES)[:, None]) % N]
    pick = np.zeros((512, 256))
    for row in range(KEEP):
        a = abs(row - HALF)
        if a < HALF:
            pick[row, 16 * (a // 8) + a % 8] = 1.0
            pick[KEEP + row, 16 * (a // 8) + 8 + a % 8] = 1.0
    flip = np.zeros((KEEP, KEEP))
    for lane in range(1, KEEP):
        flip[KEEP - lane, lane] = 1.0
    return {
        "ahead": ahead.astype(bfloat16),
        "ahead_x": ahead_x.astype(bfloat16),
        "back_x": back_x.astype(bfloat16),
        "back_y": back_y.astype(bfloat16),
        "spread": spread.astype(bfloat16),
        "spread_t": np.ascontiguousarray(spread.T).astype(bfloat16),
        "pick": pick.astype(bfloat16),
        "merge": np.ascontiguousarray(pick.T).astype(bfloat16),
        "flip": flip.astype(bfloat16),
    }


def dot_nn(left, right):
    return lax.dot_general(left, right, (((1,), (0,)), ((), ())), preferred_element_type=F32)


def dot_nt(left, right):
    return lax.dot_general(left, right, (((1,), (1,)), ((), ())), preferred_element_type=F32)


def iota(shape, axis):
    return lax.broadcasted_iota(jnp.int32, shape, axis)


def each(low, high, body):
    def step(i, carry):
        body(i)
        return carry

    lax.fori_loop(low, high, step, 0)


def place():
    tile = lax.axis_index("tile")
    mask = lax.axis_index("mask")
    pencil = lax.axis_index("pencil")
    return tile, mask, pencil, pencil // 8, pencil % 8


def remote(src, dst, send, recv, where):
    return pltpu.make_async_remote_copy(
        src_ref=src, dst_ref=dst, send_sem=send, recv_sem=recv, device_id=where, device_id_type=MESH
    )


def step_kernel(
    mask_hbm, ahead_hbm, ahead_x_hbm, back_x_hbm, back_y_hbm, spread_hbm, target_hbm, spread_t_hbm,
    pick_ref, merge_ref, flip_ref, spectra_ref, points_ref, weights_ref, radii_ref,
    gradient_hbm, scale_out, loss_out,
    mask_ref, ahead_ref, ahead_x_ref, back_x, back_y, spread, target, spread_t,
    line_ref, lines_ref, seen, kern, slices, bands, fields, gap_ref, slope_ref, hot_ref, hot_t_ref,
    part_ref, gathered, summed, pieces, whole, note, notes, totals,
    load_sem, self_sem, kz_send, kz_recv, kx_send, kx_recv, kc_send, kc_recv,
    a_send, a_recv, sz_send, sz_recv, sy_send, sy_recv,
    cy_send, cy_recv, cz_send, cz_recv, dz_send, dz_recv, dy_send, dy_recv, e_send, e_recv, f_send, f_recv,
):
    tile, mask, pencil, y, z = place()
    chip, core = (tile // 2, tile % 2)
    owner = (z >= FIRST) & (z < FIRST + 4)
    column = z - FIRST
    load_mask = pltpu.make_async_copy(mask_hbm, mask_ref, load_sem.at[0])
    load_ahead = pltpu.make_async_copy(ahead_hbm, ahead_ref, load_sem.at[1])
    load_mask.start()
    load_ahead.start()
    barrier = pltpu.get_barrier_semaphore()

    def greet(where):
        pl.semaphore_signal(barrier, inc=1, device_id=where, device_id_type=MESH)

    def spot_of(d):
        spot = (mask * 8 + tile + d) % 16
        return spot, {"mask": spot // 8, "tile": spot % 8}

    each(1, 32, lambda d: greet({"pencil": (pencil + d) % 32}))
    each(1, 16, lambda d: greet(spot_of(d)[1]))
    each(1, 8, lambda d: greet({"mask": 1 - mask, "pencil": y * 8 + (z + d) % 8}))

    sub = iota((8, KEEP), 0)
    lane = iota((8, KEEP), 1)
    freq_u = lane - HALF
    freq_v = sub + pencil * 8 - HALF
    radius = freq_u * freq_u + freq_v * freq_v
    parts = []
    for c in range(2):
        for k in range(KERN):
            limit = radii_ref[k] * radii_ref[k]
            parts.append(jnp.where(radius <= limit, spectra_ref[c, k], 0.0))
    plain = jnp.concatenate(parts, axis=0)
    turned = dot_nn(plain.astype(BF16), flip_ref[...])
    sign = jnp.where(iota((64, KEEP), 0) < 32, 1.0, -1.0)
    low = jnp.where(pencil < 16, 1.0, 0.0).astype(F32)
    plain = low * (turned * sign) + (1.0 - low) * plain
    spare = (sub == 1) & (lane == 0) & (pencil == 16)
    for part in range(8):
        rows = plain[part * 8 : part * 8 + 8]
        rest = rows - rows.astype(BF16).astype(F32)
        rows = jnp.where(spare, rest[0:1, HALF : HALF + 1], rows)
        slices[part] = jnp.concatenate([rows[:, :HALF], rows[:, HALF:]], axis=0).astype(BF16)
    kern[tile, y, z] = slices[tile]

    point_rows = points_ref[0].astype(F32) - (pencil * ROWS).astype(F32)
    point_cols = points_ref[1].astype(F32)
    normal = points_ref[2]
    step_row = jnp.where(normal == 0, 1.0, 0.0) - jnp.where(normal == 1, 1.0, 0.0)
    step_col = jnp.where(normal == 2, 1.0, 0.0) - jnp.where(normal == 3, 1.0, 0.0)
    flat = jnp.concatenate(
        [
            point_rows, point_rows - step_row, point_rows + step_row,
            point_cols, point_cols - step_col, point_cols + step_col,
            weights_ref[...], jnp.zeros((1, PTS), F32),
        ],
        axis=0,
    )
    tall = flat.T
    cols = jnp.concatenate([tall[:, 3:4], tall[:, 4:5], tall[:, 5:6]], axis=0).astype(jnp.int32)
    wide_rows = jnp.concatenate([flat[0:1], flat[1:2], flat[2:3]], axis=1).astype(jnp.int32)
    wide_cols = jnp.concatenate([flat[3:4], flat[4:5], flat[5:6]], axis=1).astype(jnp.int32)
    weight = jnp.concatenate([weights_ref[...]] * 3, axis=1)
    third = iota((1, 3 * PTS), 1)
    goal = jnp.where(third < PTS, 0.5, jnp.where(third < 2 * PTS, 1.0, 0.0))
    row_hot = jnp.where(iota((ROWS, 3 * PTS), 0) == wide_rows, 1.0, 0.0)

    load_mask.wait()
    load_ahead.wait()
    later = [
        pltpu.make_async_copy(ahead_x_hbm, ahead_x_ref, load_sem.at[2]),
        pltpu.make_async_copy(back_x_hbm.at[pencil], back_x, load_sem.at[3]),
        pltpu.make_async_copy(back_y_hbm, back_y, load_sem.at[4]),
        pltpu.make_async_copy(spread_hbm, spread, load_sem.at[5]),
        pltpu.make_async_copy(target_hbm, target, load_sem.at[6]),
        pltpu.make_async_copy(spread_t_hbm, spread_t, load_sem.at[7]),
    ]
    for load in later:
        load.start()
    line = dot_nt(ahead_ref[...], mask_ref[...].astype(BF16))
    lane8 = iota((8, ROWS), 1)
    cosine, sine = (line[256:264], line[264:272])
    both = jnp.where(lane8 < 64, cosine + pltpu.roll(cosine, 64, 1), sine + pltpu.roll(sine, 64, 1))
    empty = jnp.where(iota((8, ROWS), 0) == 0, both, line[8:16])
    line_ref[...] = jnp.concatenate([line[:8], empty, line[16:256]], axis=0).astype(BF16)

    pl.semaphore_wait(barrier, 53)

    own_lines = lines_ref.at[:, pl.ds(pl.multiple_of(pencil * ROWS, ROWS), ROWS)]

    def line_to(d):
        q = (pencil // 2 + d) % 16
        home = q // 4 * 8 + FIRST + q % 4
        src = line_ref.at[pl.ds(pl.multiple_of(q * 16, 16), 16)]
        return home, remote(src, own_lines, a_send.at[q], a_recv.at[pencil], {"pencil": home})

    def send_line(d):
        home, copy = line_to(d)

        @pl.when(home != pencil)
        def _():
            copy.start()

    each(0, 16, send_line)

    def kz(d, theirs=False):
        other = (pencil + d) % 32
        spot = other if theirs else pencil
        rows = kern.at[tile, spot // 8, spot % 8]
        return remote(rows, rows, kz_send.at[other], kz_recv.at[spot], {"pencil": other})

    each(1, 32, lambda d: kz(d).start())

    @pl.when(owner)
    def _():
        src = line_ref.at[pl.ds(pl.multiple_of((y * 4 + column) * 16, 16), 16)]
        keep = pltpu.make_async_copy(src, own_lines, self_sem)
        keep.start()
        keep.wait()

    across = jnp.broadcast_to(cols, (3 * PTS, 128)) - iota((3 * PTS, 128), 1)
    down = wide_cols - iota((128, 3 * PTS), 0)
    for base in range(0, N, 128):
        at = slice(base, base + 128)
        hot_t_ref[at, :] = jnp.where(down == base, 1.0, 0.0).astype(BF16)
        hot_ref[:, at] = jnp.where(across == base, 1.0, 0.0).astype(BF16)

    each(1, 32, lambda d: kz(d, True).wait_recv())

    def kx(d, theirs=False):
        other = (chip + d) % 4
        spot = other if theirs else chip
        rows = kern.at[spot * 2 + core]
        return remote(rows, rows, kx_send.at[other], kx_recv.at[spot], {"tile": other * 2 + core})

    def kc(d, theirs=False):
        spot = (chip + d) % 4
        rows = kern.at[spot * 2 + (1 - core if theirs else core)]
        return remote(rows, rows, kc_send.at[spot], kc_recv.at[spot], {"tile": chip * 2 + 1 - core})

    each(1, 4, lambda d: kx(d).start())
    kc(0).start()

    def sz(d):
        spot = (mask * 8 + z + d) % 16
        mine = seen.at[y, mask, column]
        where = {"mask": spot // 8, "pencil": y * 8 + spot % 8}
        return remote(mine, mine, sz_send.at[spot], sz_recv.at[mask * 4 + column], where)

    later[0].wait()

    @pl.when(owner)
    def _():
        def line_from(d):
            other = (pencil + d) % 32
            src = line_ref.at[pl.ds(0, 16)]
            dst = lines_ref.at[:, pl.ds(pl.multiple_of(other * ROWS, ROWS), ROWS)]
            return remote(src, dst, a_send.at[0], a_recv.at[other], {"pencil": other})

        each(1, 32, lambda d: line_from(d).wait_recv())
        held = lines_ref[...].astype(F32)
        first = (y == 0) & (column == 0)
        stash = (iota((16, N), 0) == 8) & first
        extra = jnp.where(stash, held, 0.0)
        left = (iota((16, N), 1) % 128) < 64
        cos_sum = jnp.sum(jnp.where(left, extra, 0.0))
        sin_sum = jnp.sum(jnp.where(left, 0.0, extra))
        out = dot_nn(jnp.where(stash, 0.0, held).astype(BF16), ahead_x_ref[...])
        real = out[:8, :KEEP] + out[8:, KEEP:]
        imag = out[8:, :KEEP] - out[:8, KEEP:]
        slot = (sub == 0) & (lane == HALF + 1) & first
        real = jnp.where(slot, cos_sum, real)
        imag = jnp.where(slot, sin_sum, imag)
        still = (sub == 0) & (lane == HALF) & first
        imag = jnp.where(still, real - real.astype(BF16).astype(F32), imag)
        piece = jnp.concatenate([real, imag], axis=0) * (1.0 / (N * N))
        seen[y, mask, column] = piece.astype(BF16)
        each(1, 16, lambda d: sz(d).start())

    def pass_on(d):
        kx(d, True).wait_recv()
        kc(d).start()

    def sz_wait(m, q):
        theirs = seen.at[y, m, q]
        mine = (m == mask) & (q == column)

        @pl.when(jnp.logical_not(mine))
        def _():
            where = {"pencil": y * 8 + (z + 1) % 8}
            remote(theirs, theirs, sz_send.at[q], sz_recv.at[m * 4 + q], where).wait_recv()

    def sy(d, m, q, theirs=False):
        other = (y + d) % 4
        spot = other if theirs else y
        rows = seen.at[spot, m, q]
        return remote(rows, rows, sy_send.at[m, other, q], sy_recv.at[m, spot, q], {"pencil": other * 8 + z})

    def near(i):
        return jnp.where(z < 4, i, 3 - i)

    def forward(m, q):
        sz_wait(m, q)
        each(1, 4, lambda d: sy(d, m, q).start())

    each(0, 4, lambda i: forward(mask, near(i)))
    each(1, 4, pass_on)
    each(0, 4, lambda i: forward(1 - mask, near(3 - i)))
    each(0, 4, lambda d: kc(d, True).wait_recv())

    slot = (sub == 0) & (lane == HALF + 1)
    still = (sub == 0) & (lane == HALF)

    for part in range(8):
        lines = kern[part].astype(F32).reshape(PENCIL, 16, HALF)
        bands[part] = jnp.concatenate(
            [lines[:, :8].reshape(KEEP, HALF), lines[:, 8:].reshape(KEEP, HALF)], axis=1
        )
        middle = bands[part, HALF : HALF + 8]
        rest = middle[1:2, 0:1]
        middle = jnp.where(still, middle + rest, jnp.where((sub == 1) & (lane == 0), 0.0, middle))
        bands[part, HALF : HALF + 8] = middle

    def spectrum(which):
        held = jnp.concatenate([seen[i, which].reshape(64, KEEP) for i in range(4)], axis=0)
        full = dot_nn(pick_ref[...], held)
        real, imag = (full[:KEEP], full[KEEP:])
        mid_real, mid_imag = (real[HALF : HALF + 8], imag[HALF : HALF + 8])
        edge_real = jnp.sum(jnp.where(slot, mid_real, 0.0))
        edge_imag = jnp.sum(jnp.where(slot, mid_imag, 0.0))
        mid_real = jnp.where(slot, pltpu.roll(mid_real, 2, 1), mid_real)
        mid_imag = jnp.where(slot, -pltpu.roll(mid_imag, 2, 1), mid_imag)
        mid_real = jnp.where(still, mid_real + mid_imag, mid_real)
        mid_imag = jnp.where(still, 0.0, mid_imag)
        top_real = jnp.where(sub == 0, edge_real, real[:8])
        top_imag = jnp.where(sub == 0, edge_imag, imag[:8])
        real = jnp.concatenate([top_real, real[8:HALF], mid_real, real[HALF + 8 :]], axis=0)
        imag = jnp.concatenate([top_imag, imag[8:HALF], mid_imag, imag[HALF + 8 :]], axis=0)
        return real, imag

    def remainder(band):
        middle = band[HALF : HALF + 8]
        return (middle - middle.astype(BF16).astype(F32))[0:1, HALF : HALF + 1]

    for load in later[1:]:
        load.wait()
    images = []
    for turn in range(2):
        which = mask if turn == 0 else 1 - mask
        each(0, 12, lambda i, which=which: sy(1 + i // 4, which, i % 4, True).wait_recv())
        real, imag = spectrum(which)
        columned, rests, rests_imag = ([], [], [])
        for k in range(KERN):
            kern_real, kern_imag = (bands[k], bands[KERN + k])
            band_real = kern_real * real - kern_imag * imag
            band_imag = kern_real * imag + kern_imag * real
            band = jnp.concatenate([band_real, band_imag], axis=1).astype(BF16)
            out = dot_nt(back_x[...], band)
            out = jnp.concatenate([out[:ROWS], out[ROWS:]], axis=1)
            rounded = out.astype(BF16)
            columned.append(rounded)
            rest = out - rounded.astype(F32)
            rests.append(rest[:, HALF : HALF + 1] + remainder(band_real))
            rests_imag.append(rest[:, KEEP + HALF : KEEP + HALF + 1] + remainder(band_imag))
        field = dot_nn(jnp.concatenate(columned, axis=0), back_y[...])
        rest_real = jnp.broadcast_to(jnp.concatenate(rests, axis=0), (512, SAMPLES))
        rest_imag = jnp.broadcast_to(jnp.concatenate(rests_imag, axis=0), (512, SAMPLES))
        field = field + jnp.concatenate([rest_real, rest_imag], axis=1)
        if turn == 0:
            fields[...] = field.astype(BF16)
        square = field * field
        square = square[:, :SAMPLES] + square[:, SAMPLES:]
        images.append(square[:128] + square[128:256] + square[256:384] + square[384:])
    image = jnp.concatenate(images, axis=0).astype(BF16)

    loss = jnp.zeros((ROWS, 128), F32)
    picked = jnp.zeros((2 * ROWS, 3 * PTS), F32)
    for base in range(0, N, CHUNK):
        at = slice(base, base + CHUNK)
        fine = dot_nn(image, spread[:, at])
        clear = 0.5 - 0.5 * jnp.tanh(3.0 * fine - 1.5)
        own, other = (clear[:ROWS], clear[ROWS:])
        product = own * other
        union = 1.0 - product
        slope_ref[:, at] = 12.0 * product * (1.0 - own)
        gap = union - target[:, at].astype(F32)
        gap_ref[:, at] = gap
        high = union.astype(BF16)
        rest = (union - high.astype(F32)).astype(BF16)
        picked = picked + dot_nn(jnp.concatenate([high, rest], axis=0), hot_t_ref[at, :])
        square = gap * gap
        loss = loss + (square[:, :128] + square[:, 128:256]) + (square[:, 256:384] + square[:, 384:])
    missed = jnp.sum((picked[:ROWS] + picked[ROWS:]) * row_hot, axis=0, keepdims=True) - goal
    push = weight * missed
    loss = jnp.sum(loss) + jnp.sum(push * missed)
    hits = (row_hot * push).astype(BF16)
    drive = jnp.zeros((ROWS, SAMPLES), F32)
    for base in range(0, N, CHUNK):
        at = slice(base, base + CHUNK)
        pull = gap_ref[:, at] + dot_nn(hits, hot_ref[:, at])
        drive = drive + dot_nn((pull * slope_ref[:, at]).astype(BF16), spread_t[at, :])
    drive = jnp.concatenate([drive, drive], axis=1)
    drive = jnp.concatenate([drive] * KERN, axis=0)
    mixed = (drive * fields[...].astype(F32)).astype(BF16)
    lines = dot_nt(back_y[...], mixed)
    sum_real = jnp.zeros((KEEP, KEEP), F32)
    sum_imag = jnp.zeros((KEEP, KEEP), F32)
    for k in range(KERN):
        at = slice(k * ROWS, (k + 1) * ROWS)
        line = jnp.concatenate([lines[:KEEP, at], lines[KEEP:, at]], axis=1).astype(BF16)
        back = dot_nn(line, back_x[...])
        back_real, back_imag = (back[:, :KEEP], back[:, KEEP:])
        kern_real, kern_imag = (bands[k], bands[KERN + k])
        sum_real = sum_real + (kern_real * back_real + kern_imag * back_imag)
        sum_imag = sum_imag + (kern_real * back_imag - kern_imag * back_real)
    sum_real = sum_real * (2.0 / (N * N))
    sum_imag = sum_imag * (2.0 / (N * N))

    mid_real, mid_imag = (sum_real[HALF : HALF + 8], sum_imag[HALF : HALF + 8])
    turned = dot_nn(jnp.concatenate([mid_real, mid_imag], axis=0).astype(BF16), flip_ref[...])
    edge_real = jnp.sum(jnp.where(still, sum_real[:8], 0.0))
    edge_imag = jnp.sum(jnp.where(still, sum_imag[:8], 0.0))
    fold_real = jnp.where(lane < HALF, mid_real + turned[:8], jnp.where(lane == HALF, mid_real, 0.0))
    fold_imag = jnp.where(lane < HALF, mid_imag - turned[8:], 0.0)
    fold_real = jnp.where(lane == HALF + 1, edge_real, jnp.where(lane == HALF + 2, loss, fold_real))
    fold_imag = jnp.where(lane == HALF + 1, edge_imag, fold_imag)
    mid_real = jnp.where(sub == 0, fold_real, mid_real)
    mid_imag = jnp.where(sub == 0, fold_imag, mid_imag)
    full = jnp.concatenate(
        [
            sum_real[:HALF], mid_real, sum_real[HALF + 8 :],
            sum_imag[:HALF], mid_imag, sum_imag[HALF + 8 :],
        ],
        axis=0,
    ).astype(BF16)
    part_ref[...] = dot_nn(merge_ref[...], full).astype(BF16).reshape(4, 4, 16, KEEP)

    def far(i):
        return near(3 - i)

    def cy(d, q, theirs=False):
        other = (y + d) % 4
        spot = other if theirs else y
        where = {"pencil": other * 8 + z}
        return remote(part_ref.at[other, q], gathered.at[spot, q], cy_send.at[other, q], cy_recv.at[spot, q], where)

    each(0, 12, lambda i: cy(1 + i % 3, far(i // 3)).start())
    gathered[y] = part_ref[y]

    def cz(q):
        home = FIRST + q
        return home, remote(summed.at[q], pieces.at[z], cz_send.at[q], cz_recv.at[z], {"pencil": y * 8 + home})

    def add_piece(i):
        q = far(i)
        each(1, 4, lambda d: cy(d, q, True).wait_recv())
        total = gathered[0, q].astype(F32) + gathered[1, q].astype(F32)
        total = total + (gathered[2, q].astype(F32) + gathered[3, q].astype(F32))
        summed[q] = total.astype(BF16)
        home, copy = cz(q)

        @pl.when(home != z)
        def _():
            copy.start()

    each(0, 4, add_piece)

    def dz(d):
        other = (z + d) % 8
        mine = whole.at[y, column]
        return remote(mine, mine, dz_send.at[other], dz_recv.at[column], {"pencil": y * 8 + other})

    row = iota((16, KEEP), 0)
    lane = iota((16, KEEP), 1)
    note_row = iota((8, 128), 0)
    here = mask * 8 + tile

    def tell(d):
        spot, where = spot_of(d)
        return remote(note, notes.at[here], e_send.at[spot], e_recv.at[here], where)

    def told(d):
        spot, where = spot_of(d)
        return remote(note, notes.at[spot], e_send.at[spot], e_recv.at[spot], where)

    @pl.when(owner)
    def _():
        pieces[z] = summed[column]

        def piece_from(d):
            other = (z + d) % 8
            where = {"pencil": y * 8 + other}
            return remote(summed.at[0], pieces.at[other], cz_send.at[0], cz_recv.at[other], where)

        each(1, 8, lambda d: piece_from(d).wait_recv())
        one = pieces[...].astype(F32)
        one = (one[0] + one[1]) + (one[2] + one[3]) + (one[4] + one[5]) + (one[6] + one[7])
        whole[y, column] = one.astype(BF16)
        each(1, 8, lambda d: dz(d).start())
        first = (y == 0) & (column == 0)
        loss = jnp.sum(jnp.where(first & (row == 0) & (lane == HALF + 2), one, 0.0))
        stash = first & ((row == 0) | (row == 8)) & (lane > HALF + 1)
        center = first & (row == 0) & (lane == HALF)
        energy = jnp.where(stash, 0.0, one * one) * jnp.where(center, 1.0, 0.5)
        energy = jnp.sum(energy)
        note[...] = jnp.where(note_row == 0, energy, jnp.where(note_row == 1, loss, 0.0))
        each(1, 16, lambda d: tell(d).start())
        notes[here] = note[...]

    def dz_wait(q):
        theirs = whole.at[y, q]

        @pl.when(q != column)
        def _():
            where = {"pencil": y * 8 + (z + 1) % 8}
            remote(theirs, theirs, dz_send.at[q], dz_recv.at[q], where).wait_recv()

    def dy(d, q, theirs=False):
        other = (y + d) % 4
        spot = other if theirs else y
        rows = whole.at[spot, q]
        return remote(rows, rows, dy_send.at[other, q], dy_recv.at[spot, q], {"pencil": other * 8 + z})

    def forward_piece(i):
        q = near(i)
        dz_wait(q)
        each(1, 4, lambda d: dy(d, q).start())

    each(0, 4, forward_piece)

    def share(d):
        other = (pencil + d) % 32
        mine = totals.at[y * 4 + column]
        return remote(mine, mine, f_send.at[other], f_recv.at[y * 4 + column], {"pencil": other})

    @pl.when(owner)
    def _():
        each(1, 16, lambda d: told(d).wait_recv())
        total = notes[0]
        for spot in range(1, 16):
            total = total + notes[spot]
        totals[y * 4 + column] = total
        each(1, 32, lambda d: share(d).start())

    each(0, 12, lambda i: dy(1 + i // 4, i % 4, True).wait_recv())

    band = whole[...].astype(F32).reshape(KEEP, KEEP)
    head = band[:16]
    edge_real = jnp.sum(jnp.where((row == 0) & (lane == HALF + 1), head, 0.0))
    edge_imag = jnp.sum(jnp.where((row == 8) & (lane == HALF + 1), head, 0.0))
    head = jnp.where(((row == 0) | (row == 8)) & (lane > HALF), 0.0, head)
    band = jnp.concatenate([head, band[16:]], axis=0)
    pairs = band.reshape(16, 2, 8, KEEP)
    turned = jnp.concatenate([pairs[:, 1:2], -pairs[:, 0:1]], axis=1).reshape(KEEP, KEEP)
    stacked = jnp.concatenate([band, turned], axis=1).astype(BF16)
    lines = dot_nt(back_x[0:ROWS], stacked).astype(BF16)
    for base in range(0, N, CHUNK):
        at = slice(base, base + CHUNK)
        extra = ahead_ref[256:272, at].astype(F32)
        extra = edge_real * extra[0:1] + edge_imag * extra[8:9]
        target[:, at] = (dot_nn(lines, ahead_ref[0:256, at]) + extra).astype(BF16)
    store = pltpu.make_async_copy(target, gradient_hbm, load_sem.at[0])
    store.start()

    each(1, 32, lambda d: kz(d).wait_send())
    each(1, 4, lambda d: kx(d).wait_send())
    each(0, 4, lambda d: kc(d).wait_send())
    each(0, 12, lambda i: sy(1 + i // 4, 0, i % 4).wait_send())
    each(0, 12, lambda i: sy(1 + i // 4, 1, i % 4).wait_send())
    each(0, 12, lambda i: cy(1 + i // 4, i % 4).wait_send())
    each(0, 12, lambda i: dy(1 + i // 4, i % 4).wait_send())

    def sent_line(d):
        home, copy = line_to(d)

        @pl.when(home != pencil)
        def _():
            copy.wait_send()

    each(0, 16, sent_line)

    def sent_piece(q):
        home, copy = cz(q)

        @pl.when(home != z)
        def _():
            copy.wait_send()

    each(0, 4, sent_piece)

    @pl.when(owner)
    def _():
        each(1, 16, lambda d: sz(d).wait_send())
        each(1, 8, lambda d: dz(d).wait_send())

    def share_wait(q):
        theirs = totals.at[q]
        home = q // 4 * 8 + FIRST + q % 4

        @pl.when(home != pencil)
        def _():
            where = {"pencil": (pencil + 1) % 32}
            remote(theirs, theirs, f_send.at[q], f_recv.at[q], where).wait_recv()

    each(0, 16, share_wait)
    total = totals[0]
    for q in range(1, 16):
        total = total + totals[q]
    scale_out[...] = STEP_SIZE * lax.rsqrt(total[0:1] * (1.0 / 16.0) + EPSILON)
    loss_out[0, 0] = jnp.sum(jnp.where(note_row == 1, total, 0.0)) * (0.5 / (128.0 * 8.0 * N * N))
    store.wait()

    @pl.when(owner)
    def _():
        each(1, 16, lambda d: tell(d).wait_send())
        each(1, 32, lambda d: share(d).wait_send())


ANY_SPEC = pl.BlockSpec(memory_space=pl.ANY)
VMEM_SPEC = pl.BlockSpec(memory_space=VMEM)
SMEM_SPEC = pl.BlockSpec(memory_space=pltpu.SMEM)
LIMIT = 56 * 1024 * 1024


def per_device(mask_field, design_target, kernel_spectra, support_radii, edge_points, point_weights):
    table = {name: jnp.asarray(value) for name, value in tables().items()}
    plane = mask_field.reshape(ROWS, N)
    gradient, scale, loss = pl.pallas_call(
        step_kernel,
        out_shape=(
            jax.ShapeDtypeStruct((ROWS, N), BF16),
            jax.ShapeDtypeStruct((1, 128), F32),
            jax.ShapeDtypeStruct((1, 1), F32),
        ),
        in_specs=[ANY_SPEC] * 8 + [VMEM_SPEC] * 6 + [SMEM_SPEC],
        out_specs=(ANY_SPEC, VMEM_SPEC, SMEM_SPEC),
        scratch_shapes=[
            VMEM((ROWS, N), F32),
            VMEM((272, N), BF16),
            VMEM((N, 512), BF16),
            VMEM((256, 512), BF16),
            VMEM((512, 1024), BF16),
            VMEM((SAMPLES, N), BF16),
            VMEM((ROWS, N), BF16),
            VMEM((N, SAMPLES), BF16),
            VMEM((256, ROWS), BF16),
            VMEM((16, N), BF16),
            VMEM((4, 2, 4, 16, KEEP), BF16),
            VMEM((8, 4, 8, 16, HALF), BF16),
            VMEM((8, 16, HALF), BF16),
            VMEM((8, KEEP, KEEP), F32),
            VMEM((512, 1024), BF16),
            VMEM((ROWS, N), F32),
            VMEM((ROWS, N), F32),
            VMEM((3 * PTS, N), BF16),
            VMEM((N, 3 * PTS), BF16),
            VMEM((4, 4, 16, KEEP), BF16),
            VMEM((4, 4, 16, KEEP), BF16),
            VMEM((4, 16, KEEP), BF16),
            VMEM((8, 16, KEEP), BF16),
            VMEM((4, 4, 16, KEEP), BF16),
            VMEM((8, 128), F32),
            VMEM((16, 8, 128), F32),
            VMEM((16, 8, 128), F32),
            DMA((8,)),
            DMA,
        ]
        + [DMA((32,))] * 2
        + [DMA((4,))] * 4
        + [DMA((16,)), DMA((32,)), DMA((16,)), DMA((8,)), DMA((2, 4, 4)), DMA((2, 4, 4))]
        + [DMA((4, 4)), DMA((4, 4)), DMA((4,)), DMA((8,)), DMA((8,)), DMA((4,)), DMA((4, 4)), DMA((4, 4))]
        + [DMA((16,)), DMA((16,)), DMA((32,)), DMA((16,))],
        compiler_params=pltpu.CompilerParams(collective_id=0, has_side_effects=True, vmem_limit_bytes=LIMIT),
        name="step_kernel",
    )(
        plane, table["ahead"], table["ahead_x"], table["back_x"], table["back_y"], table["spread"],
        design_target.reshape(ROWS, N), table["spread_t"], table["pick"], table["merge"], table["flip"],
        kernel_spectra, edge_points.reshape(3, 1, PTS), point_weights, support_radii,
    )
    update = (plane - scale[0, 0] * gradient.astype(F32)).astype(BF16)
    return update.reshape(1, 1, ROWS, N), loss.reshape(())


def solution(mesh):
    placed = (
        P("tile", "mask", "pencil", None),
        P("tile", "pencil", None),
        P(None, None, "pencil", None),
        P(),
        P("tile", None, "pencil"),
        P("tile", "pencil"),
    )
    return jax.shard_map(
        per_device,
        mesh=mesh,
        in_specs=placed,
        out_specs=(P("tile", "mask", "pencil", None), P()),
        check_vma=False,
    )
```

time: 524 us -> 88.2 us (0.17)
  blocking collectives: 180 us -> 0 us
  local copies, waits for them, and re-layouts: 104 us -> 0.01 us
  waiting for transfers between devices: 96.7 us -> 0 us
  Pallas kernels: 0 us -> 82.5 us
  matrix products: 64.6 us -> 0 us
  other arithmetic: 38.5 us -> 3.1 us
  starting transfers between devices: 29.8 us -> 0 us
    psum x1 -> x0, blocking collectives: 103 us -> none  [per_device(): square_total = lax.psum(squares, ('tile', 'mask', 'pencil'))]
    ppermute x1 -> x0, waiting for transfers between devices: 82.6 us -> none  [partner_2(): return lax.ppermute(block, axis, route)]
    pallas_call x0 -> x1, Pallas kernels: none -> 82.5 us  [per_device(): pl.pallas_call(step_kernel, out_shape=(jax.ShapeDtypeStruct((ROWS, N), BF...]
    all_to_all x2 -> x0, blocking collectives: 76.8 us -> none  [the longest x1 39.2 us: per_device(): lax.all_to_all(adjoint_lines, 'pencil', split_axis=2, concat_axis=3, tile...]
    dot_general x16 -> x0, matrix products: 64.6 us -> none  [contract(): return jnp.einsum(form, left, right, preferred_element_type=jnp.float32)]
    unnamed x29 -> x2, local copies, waits for them, and re-layouts: 42.1 us -> 0.01 us
    all_to_all x2 -> x0, starting transfers between devices: 21.8 us -> none  [the longest x1 16.4 us: per_device(): lax.all_to_all(lined, 'pencil', split_axis=2, concat_axis=3, tiled=True)]
    convert_element_type x8 -> x0, local copies, waits for them, and re-layouts: 17.1 us -> none  [the longest x1 9.41 us: per_device(): inverse_pass(band_data, tables, False, 2).astype(jnp.bfloat16)]
  transfers between devices with their start and end apart: 3 -> 0, of which waited for: 3 -> 0; matrix products, arithmetic and copies ran while one was open for 3% -> 0% of each run, Pallas kernels for 0% -> 0%
where the time goes in v1:
time: 88.2 us; the launch traced here: 88 us
  Pallas kernels  82.5 us (94%)
  other arithmetic  3.1 us (4%)
  between operations  2.42 us (3%)
    pallas_call x1, Pallas kernels, per_device(): pl.pallas_call(step_kernel, out_shape=(jax.ShapeDtypeStruct((ROWS, N), BF...  82.5 us
    reshape x1, other arithmetic, per_device(): return (update.reshape(1, 1, ROWS, N), loss.reshape(()))  3.1 us

profile of v1, /device:TPU:1, one launch (start us, length us, event | category | flops | bytes accessed | tf_op | source)
XLA Modules:
  0.0 88.0 jit_solution(12607074393332105552)
XLA Ops:
  0.6 0.0 copy-start
  0.6 82.5 %step_kernel.1 = (bf16[128,4096]{1,0:T(8,128)(2,1)}, f32[1,128]{1,0:T(1,128)}, f32[1,1]{1,0:T(1,128)}) custom-call(f32[128,4096]{1,0:T(8,128)} %bitcast.9, bf16[272,4096]{1,0:T(8,128)(2,1)} %constant.18.clone.ahead_hbm, bf16[4096,512]{1,0:T(8,128)(2,1)} %constant.19.clone.ahead_x_hbm, bf16[32,256,512]{2,1,0:T(8,128)(2,1)} %constant.20.clone.back_x_hbm, ...), custom_call_target="tpu_custom_call" | custom-call | tf_op jit(solution)/shard_map/step_kernel/pallas_call | solution.py:663
  83.1 0.0 copy-done
  83.2 3.1 %fusion = bf16[1,1,128,4096]{3,2,1,0:T(8,128)(2,1)} fusion(bf16[128,4096]{1,0:T(8,128)(2,1)} %get-tuple-element.6, f32[]{:T(128)} %bitcast.12, f32[1,1,128,4096]{3,2,1,0:T(8,128)S(1)} %copy-done), kind=kLoop, calls=%fused_computation.1 | loop fusion | flops 2097152 | bytes 4194308 | tf_op jit(solution)/shard_map/reshape | solution.py:716
Async XLA Ops:
  0.6 82.5 %copy-start = (f32[1,1,128,4096]{3,2,1,0:T(8,128)S(1)}, f32[1,1,128,4096]{3,2,1,0:T(8,128)}, u32[]{:S(2)}) copy-start(f32[1,1,128,4096]{3,2,1,0:T(8,128)} %param.15) | copy-start | bytes 6291460

commit v2 on v1

--- a/solution.py
+++ b/solution.py
@@ -130,7 +130,7 @@
     mask_ref, ahead_ref, ahead_x_ref, back_x, back_y, spread, target, spread_t,
     line_ref, lines_ref, seen, kern, slices, bands, fields, gap_ref, slope_ref, hot_ref, hot_t_ref,
     part_ref, gathered, summed, pieces, whole, note, notes, totals,
-    load_sem, self_sem, kz_send, kz_recv, kx_send, kx_recv, kc_send, kc_recv,
+    load_sem, self_sem, kz_send, kz_recv, ka_send, ka_recv, kb_send, kb_recv, kd_send, kd_recv, ke_send, ke_recv, kc_send, kc_recv,
     a_send, a_recv, sz_send, sz_recv, sy_send, sy_recv,
     cy_send, cy_recv, cz_send, cz_recv, dz_send, dz_recv, dy_send, dy_recv, e_send, e_recv, f_send, f_recv,
 ):
@@ -176,7 +176,7 @@
         rest = rows - rows.astype(BF16).astype(F32)
         rows = jnp.where(spare, rest[0:1, HALF : HALF + 1], rows)
         slices[part] = jnp.concatenate([rows[:, :HALF], rows[:, HALF:]], axis=0).astype(BF16)
-    kern[tile, y, z] = slices[tile]
+    kern[core, chip, y, z] = slices[tile]
 
     point_rows = points_ref[0].astype(F32) - (pencil * ROWS).astype(F32)
     point_cols = points_ref[1].astype(F32)
@@ -221,6 +221,45 @@
 
     pl.semaphore_wait(barrier, 53)
 
+    def hop(rows, send, recv, other, spot, where):
+        return remote(rows, rows, send.at[other], recv.at[spot], where)
+
+    def kz(d, theirs=False):
+        other = (z + d) % 8
+        spot = other if theirs else z
+        return hop(kern.at[core, chip, y, spot], kz_send, kz_recv, other, spot, {"pencil": y * 8 + other})
+
+    def along_x(d, theirs):
+        other = (chip + d) % 4
+        return other, other if theirs else chip, {"tile": other * 2 + core}
+
+    def along_y(d, theirs):
+        other = (y + d) % 4
+        return other, other if theirs else y, {"pencil": other * 8 + z}
+
+    def ka(d, theirs=False):
+        other, spot, where = along_x(d, theirs)
+        return hop(kern.at[core, spot, y, pl.ds(0, 4)], ka_send, ka_recv, other, spot, where)
+
+    def kb(d, theirs=False):
+        other, spot, where = along_y(d, theirs)
+        return hop(kern.at[core, chip, spot, pl.ds(4, 4)], kb_send, kb_recv, other, spot, where)
+
+    def kd(d, theirs=False):
+        other, spot, where = along_y(d, theirs)
+        return hop(kern.at[core, pl.ds(0, 4), spot, pl.ds(0, 4)], kd_send, kd_recv, other, spot, where)
+
+    def ke(d, theirs=False):
+        other, spot, where = along_x(d, theirs)
+        return hop(kern.at[core, spot, pl.ds(0, 4), pl.ds(4, 4)], ke_send, ke_recv, other, spot, where)
+
+    def kc(half, theirs=False):
+        side = 1 - core if theirs else core
+        rows = kern.at[side, pl.ds(0, 4), pl.ds(0, 4), pl.ds(4 * half, 4)]
+        return remote(rows, rows, kc_send.at[half], kc_recv.at[half], {"tile": chip * 2 + 1 - core})
+
+    each(1, 8, lambda d: kz(d).start())
+
     own_lines = lines_ref.at[:, pl.ds(pl.multiple_of(pencil * ROWS, ROWS), ROWS)]
 
     def line_to(d):
@@ -237,14 +276,6 @@
             copy.start()
 
     each(0, 16, send_line)
-
-    def kz(d, theirs=False):
-        other = (pencil + d) % 32
-        spot = other if theirs else pencil
-        rows = kern.at[tile, spot // 8, spot % 8]
-        return remote(rows, rows, kz_send.at[other], kz_recv.at[spot], {"pencil": other})
-
-    each(1, 32, lambda d: kz(d).start())
 
     @pl.when(owner)
     def _():
@@ -253,28 +284,18 @@
         keep.start()
         keep.wait()
 
-    across = jnp.broadcast_to(cols, (3 * PTS, 128)) - iota((3 * PTS, 128), 1)
+    each(1, 8, lambda d: kz(d, True).wait_recv())
+    each(1, 4, lambda d: ka(d).start())
+    each(1, 4, lambda d: kb(d).start())
+
     down = wide_cols - iota((128, 3 * PTS), 0)
     for base in range(0, N, 128):
-        at = slice(base, base + 128)
-        hot_t_ref[at, :] = jnp.where(down == base, 1.0, 0.0).astype(BF16)
-        hot_ref[:, at] = jnp.where(across == base, 1.0, 0.0).astype(BF16)
-
-    each(1, 32, lambda d: kz(d, True).wait_recv())
-
-    def kx(d, theirs=False):
-        other = (chip + d) % 4
-        spot = other if theirs else chip
-        rows = kern.at[spot * 2 + core]
-        return remote(rows, rows, kx_send.at[other], kx_recv.at[spot], {"tile": other * 2 + core})
-
-    def kc(d, theirs=False):
-        spot = (chip + d) % 4
-        rows = kern.at[spot * 2 + (1 - core if theirs else core)]
-        return remote(rows, rows, kc_send.at[spot], kc_recv.at[spot], {"tile": chip * 2 + 1 - core})
-
-    each(1, 4, lambda d: kx(d).start())
-    kc(0).start()
+        hot_t_ref[base : base + 128, :] = jnp.where(down == base, 1.0, 0.0).astype(BF16)
+
+    each(1, 4, lambda d: ka(d, True).wait_recv())
+    each(1, 4, lambda d: kd(d).start())
+    each(1, 4, lambda d: kb(d, True).wait_recv())
+    each(1, 4, lambda d: ke(d).start())
 
     def sz(d):
         spot = (mask * 8 + z + d) % 16
@@ -312,9 +333,14 @@
         seen[y, mask, column] = piece.astype(BF16)
         each(1, 16, lambda d: sz(d).start())
 
-    def pass_on(d):
-        kx(d, True).wait_recv()
-        kc(d).start()
+    across = jnp.broadcast_to(cols, (3 * PTS, 128)) - iota((3 * PTS, 128), 1)
+    for base in range(0, N, 128):
+        hot_ref[:, base : base + 128] = jnp.where(across == base, 1.0, 0.0).astype(BF16)
+
+    each(1, 4, lambda d: kd(d, True).wait_recv())
+    kc(0).start()
+    each(1, 4, lambda d: ke(d, True).wait_recv())
+    kc(1).start()
 
     def sz_wait(m, q):
         theirs = seen.at[y, m, q]
@@ -339,15 +365,15 @@
         each(1, 4, lambda d: sy(d, m, q).start())
 
     each(0, 4, lambda i: forward(mask, near(i)))
-    each(1, 4, pass_on)
     each(0, 4, lambda i: forward(1 - mask, near(3 - i)))
-    each(0, 4, lambda d: kc(d, True).wait_recv())
+    kc(0, True).wait_recv()
+    kc(1, True).wait_recv()
 
     slot = (sub == 0) & (lane == HALF + 1)
     still = (sub == 0) & (lane == HALF)
 
     for part in range(8):
-        lines = kern[part].astype(F32).reshape(PENCIL, 16, HALF)
+        lines = kern[part % 2, part // 2].astype(F32).reshape(PENCIL, 16, HALF)
         bands[part] = jnp.concatenate(
             [lines[:, :8].reshape(KEEP, HALF), lines[:, 8:].reshape(KEEP, HALF)], axis=1
         )
@@ -597,9 +623,11 @@
     store = pltpu.make_async_copy(target, gradient_hbm, load_sem.at[0])
     store.start()
 
-    each(1, 32, lambda d: kz(d).wait_send())
-    each(1, 4, lambda d: kx(d).wait_send())
-    each(0, 4, lambda d: kc(d).wait_send())
+    each(1, 8, lambda d: kz(d).wait_send())
+    for step in (ka, kb, kd, ke):
+        each(1, 4, lambda d, step=step: step(d).wait_send())
+    kc(0).wait_send()
+    kc(1).wait_send()
     each(0, 12, lambda i: sy(1 + i // 4, 0, i % 4).wait_send())
     each(0, 12, lambda i: sy(1 + i // 4, 1, i % 4).wait_send())
     each(0, 12, lambda i: cy(1 + i // 4, i % 4).wait_send())
@@ -681,7 +709,7 @@
             VMEM((256, ROWS), BF16),
             VMEM((16, N), BF16),
             VMEM((4, 2, 4, 16, KEEP), BF16),
-            VMEM((8, 4, 8, 16, HALF), BF16),
+            VMEM((2, 4, 4, 8, 16, HALF), BF16),
             VMEM((8, 16, HALF), BF16),
             VMEM((8, KEEP, KEEP), F32),
             VMEM((512, 1024), BF16),
@@ -700,8 +728,9 @@
             DMA((8,)),
             DMA,
         ]
-        + [DMA((32,))] * 2
-        + [DMA((4,))] * 4
+        + [DMA((8,))] * 2
+        + [DMA((4,))] * 8
+        + [DMA((2,))] * 2
         + [DMA((16,)), DMA((32,)), DMA((16,)), DMA((8,)), DMA((2, 4, 4)), DMA((2, 4, 4))]
         + [DMA((4, 4)), DMA((4, 4)), DMA((4,)), DMA((8,)), DMA((8,)), DMA((4,)), DMA((4, 4)), DMA((4, 4))]
         + [DMA((16,)), DMA((16,)), DMA((32,)), DMA((16,))],

time: 88.2 us -> 85.4 us (0.968)
  Pallas kernels: 82.5 us -> 79.6 us
    pallas_call x1, Pallas kernels: 82.5 us -> 79.6 us  [per_device(): pl.pallas_call(step_kernel, out_shape=(jax.ShapeDtypeStruct((ROWS, N), BF...]
where the time goes in v2:
time: 85.4 us; the launch traced here: 85.2 us
  Pallas kernels  79.6 us (93%)
  other arithmetic  3.1 us (4%)
  between operations  2.42 us (3%)
    pallas_call x1, Pallas kernels, per_device(): pl.pallas_call(step_kernel, out_shape=(jax.ShapeDtypeStruct((ROWS, N), BF...  79.6 us
    reshape x1, other arithmetic, per_device(): return (update.reshape(1, 1, ROWS, N), loss.reshape(()))  3.1 us

profile of v2, /device:TPU:1, one launch (start us, length us, event | category | flops | bytes accessed | tf_op | source)
XLA Modules:
  0.0 85.2 jit_solution(14439962796680771072)
XLA Ops:
  0.6 0.0 copy-start
  0.6 79.6 %step_kernel.1 = (bf16[128,4096]{1,0:T(8,128)(2,1)}, f32[1,128]{1,0:T(1,128)}, f32[1,1]{1,0:T(1,128)}) custom-call(f32[128,4096]{1,0:T(8,128)} %bitcast.9, bf16[272,4096]{1,0:T(8,128)(2,1)} %constant.18.clone.ahead_hbm, bf16[4096,512]{1,0:T(8,128)(2,1)} %constant.19.clone.ahead_x_hbm, bf16[32,256,512]{2,1,0:T(8,128)(2,1)} %constant.20.clone.back_x_hbm, ...), custom_call_target="tpu_custom_call" | custom-call | tf_op jit(solution)/shard_map/step_kernel/pallas_call | solution.py:691
  80.3 0.0 copy-done
  80.3 3.1 %fusion = bf16[1,1,128,4096]{3,2,1,0:T(8,128)(2,1)} fusion(bf16[128,4096]{1,0:T(8,128)(2,1)} %get-tuple-element.6, f32[]{:T(128)} %bitcast.12, f32[1,1,128,4096]{3,2,1,0:T(8,128)S(1)} %copy-done), kind=kLoop, calls=%fused_computation.1 | loop fusion | flops 2097152 | bytes 4194308 | tf_op jit(solution)/shard_map/reshape | solution.py:745
Async XLA Ops:
  0.6 79.7 %copy-start = (f32[1,1,128,4096]{3,2,1,0:T(8,128)S(1)}, f32[1,1,128,4096]{3,2,1,0:T(8,128)}, u32[]{:S(2)}) copy-start(f32[1,1,128,4096]{3,2,1,0:T(8,128)} %param.15) | copy-start | bytes 6291460

commit v3 on v2

--- a/solution.py
+++ b/solution.py
@@ -129,10 +129,10 @@
     gradient_hbm, scale_out, loss_out,
     mask_ref, ahead_ref, ahead_x_ref, back_x, back_y, spread, target, spread_t,
     line_ref, lines_ref, seen, kern, slices, bands, fields, gap_ref, slope_ref, hot_ref, hot_t_ref,
-    part_ref, gathered, summed, pieces, whole, note, notes, totals,
+    part_ref, gathered, summed, pieces, whole, note, notes, rounds, totals,
     load_sem, self_sem, kz_send, kz_recv, ka_send, ka_recv, kb_send, kb_recv, kd_send, kd_recv, ke_send, ke_recv, kc_send, kc_recv,
     a_send, a_recv, sz_send, sz_recv, sy_send, sy_recv,
-    cy_send, cy_recv, cz_send, cz_recv, dz_send, dz_recv, dy_send, dy_recv, e_send, e_recv, f_send, f_recv,
+    cy_send, cy_recv, cz_send, cz_recv, dz_send, dz_recv, dy_send, dy_recv, e_send, e_recv, f_send, f_recv, g_send, g_recv,
 ):
     tile, mask, pencil, y, z = place()
     chip, core = (tile // 2, tile % 2)
@@ -147,13 +147,9 @@
     def greet(where):
         pl.semaphore_signal(barrier, inc=1, device_id=where, device_id_type=MESH)
 
-    def spot_of(d):
-        spot = (mask * 8 + tile + d) % 16
-        return spot, {"mask": spot // 8, "tile": spot % 8}
-
     each(1, 32, lambda d: greet({"pencil": (pencil + d) % 32}))
-    each(1, 16, lambda d: greet(spot_of(d)[1]))
-    each(1, 8, lambda d: greet({"mask": 1 - mask, "pencil": y * 8 + (z + d) % 8}))
+    each(0, 8, lambda d: greet({"mask": 1 - mask, "pencil": y * 8 + d}))
+    each(1, 8, lambda d: greet({"tile": (tile + d) % 8}))
 
     sub = iota((8, KEEP), 0)
     lane = iota((8, KEEP), 1)
@@ -219,7 +215,7 @@
     empty = jnp.where(iota((8, ROWS), 0) == 0, both, line[8:16])
     line_ref[...] = jnp.concatenate([line[:8], empty, line[16:256]], axis=0).astype(BF16)
 
-    pl.semaphore_wait(barrier, 53)
+    pl.semaphore_wait(barrier, 46)
 
     def hop(rows, send, recv, other, spot, where):
         return remote(rows, rows, send.at[other], recv.at[spot], where)
@@ -351,21 +347,18 @@
             where = {"pencil": y * 8 + (z + 1) % 8}
             remote(theirs, theirs, sz_send.at[q], sz_recv.at[m * 4 + q], where).wait_recv()
 
-    def sy(d, m, q, theirs=False):
+    def sy(d, m, theirs=False):
         other = (y + d) % 4
         spot = other if theirs else y
-        rows = seen.at[spot, m, q]
-        return remote(rows, rows, sy_send.at[m, other, q], sy_recv.at[m, spot, q], {"pencil": other * 8 + z})
-
-    def near(i):
-        return jnp.where(z < 4, i, 3 - i)
-
-    def forward(m, q):
-        sz_wait(m, q)
-        each(1, 4, lambda d: sy(d, m, q).start())
-
-    each(0, 4, lambda i: forward(mask, near(i)))
-    each(0, 4, lambda i: forward(1 - mask, near(3 - i)))
+        rows = seen.at[spot, m]
+        return remote(rows, rows, sy_send.at[m, other], sy_recv.at[m, spot], {"pencil": other * 8 + z})
+
+    def forward(m):
+        each(0, 4, lambda q: sz_wait(m, q))
+        each(1, 4, lambda d: sy(d, m).start())
+
+    forward(mask)
+    forward(1 - mask)
     kc(0, True).wait_recv()
     kc(1, True).wait_recv()
 
@@ -408,7 +401,7 @@
     images = []
     for turn in range(2):
         which = mask if turn == 0 else 1 - mask
-        each(0, 12, lambda i, which=which: sy(1 + i // 4, which, i % 4, True).wait_recv())
+        each(1, 4, lambda d, which=which: sy(d, which, True).wait_recv())
         real, imag = spectrum(which)
         columned, rests, rests_imag = ([], [], [])
         for k in range(KERN):
@@ -496,35 +489,31 @@
     ).astype(BF16)
     part_ref[...] = dot_nn(merge_ref[...], full).astype(BF16).reshape(4, 4, 16, KEEP)
 
-    def far(i):
-        return near(3 - i)
-
-    def cy(d, q, theirs=False):
+    def cy(d, theirs=False):
         other = (y + d) % 4
         spot = other if theirs else y
         where = {"pencil": other * 8 + z}
-        return remote(part_ref.at[other, q], gathered.at[spot, q], cy_send.at[other, q], cy_recv.at[spot, q], where)
-
-    each(0, 12, lambda i: cy(1 + i % 3, far(i // 3)).start())
+        return remote(part_ref.at[other], gathered.at[spot], cy_send.at[other], cy_recv.at[spot], where)
+
+    each(1, 4, lambda d: cy(d).start())
     gathered[y] = part_ref[y]
+    each(1, 4, lambda d: cy(d, True).wait_recv())
+    total = gathered[0].astype(F32) + gathered[1].astype(F32)
+    total = total + (gathered[2].astype(F32) + gathered[3].astype(F32))
+    summed[...] = total.astype(BF16)
 
     def cz(q):
         home = FIRST + q
         return home, remote(summed.at[q], pieces.at[z], cz_send.at[q], cz_recv.at[z], {"pencil": y * 8 + home})
 
-    def add_piece(i):
-        q = far(i)
-        each(1, 4, lambda d: cy(d, q, True).wait_recv())
-        total = gathered[0, q].astype(F32) + gathered[1, q].astype(F32)
-        total = total + (gathered[2, q].astype(F32) + gathered[3, q].astype(F32))
-        summed[q] = total.astype(BF16)
+    def send_piece(q):
         home, copy = cz(q)
 
         @pl.when(home != z)
         def _():
             copy.start()
 
-    each(0, 4, add_piece)
+    each(0, 4, send_piece)
 
     def dz(d):
         other = (z + d) % 8
@@ -534,15 +523,11 @@
     row = iota((16, KEEP), 0)
     lane = iota((16, KEEP), 1)
     note_row = iota((8, 128), 0)
-    here = mask * 8 + tile
-
-    def tell(d):
-        spot, where = spot_of(d)
-        return remote(note, notes.at[here], e_send.at[spot], e_recv.at[here], where)
-
-    def told(d):
-        spot, where = spot_of(d)
-        return remote(note, notes.at[spot], e_send.at[spot], e_recv.at[spot], where)
+
+    def tell(d, theirs=False):
+        other = (tile + d) % 8
+        spot = other if theirs else tile
+        return remote(note, notes.at[spot], e_send.at[other], e_recv.at[spot], {"tile": other})
 
     @pl.when(owner)
     def _():
@@ -557,7 +542,6 @@
         one = pieces[...].astype(F32)
         one = (one[0] + one[1]) + (one[2] + one[3]) + (one[4] + one[5]) + (one[6] + one[7])
         whole[y, column] = one.astype(BF16)
-        each(1, 8, lambda d: dz(d).start())
         first = (y == 0) & (column == 0)
         loss = jnp.sum(jnp.where(first & (row == 0) & (lane == HALF + 2), one, 0.0))
         stash = first & ((row == 0) | (row == 8)) & (lane > HALF + 1)
@@ -565,8 +549,9 @@
         energy = jnp.where(stash, 0.0, one * one) * jnp.where(center, 1.0, 0.5)
         energy = jnp.sum(energy)
         note[...] = jnp.where(note_row == 0, energy, jnp.where(note_row == 1, loss, 0.0))
-        each(1, 16, lambda d: tell(d).start())
-        notes[here] = note[...]
+        each(1, 8, lambda d: tell(d).start())
+        notes[tile] = note[...]
+        each(1, 8, lambda d: dz(d).start())
 
     def dz_wait(q):
         theirs = whole.at[y, q]
@@ -576,34 +561,47 @@
             where = {"pencil": y * 8 + (z + 1) % 8}
             remote(theirs, theirs, dz_send.at[q], dz_recv.at[q], where).wait_recv()
 
-    def dy(d, q, theirs=False):
+    def dy(d, theirs=False):
         other = (y + d) % 4
         spot = other if theirs else y
-        rows = whole.at[spot, q]
-        return remote(rows, rows, dy_send.at[other, q], dy_recv.at[spot, q], {"pencil": other * 8 + z})
-
-    def forward_piece(i):
-        q = near(i)
-        dz_wait(q)
-        each(1, 4, lambda d: dy(d, q).start())
-
-    each(0, 4, forward_piece)
+        rows = whole.at[spot]
+        return remote(rows, rows, dy_send.at[other], dy_recv.at[spot], {"pencil": other * 8 + z})
 
     def share(d):
-        other = (pencil + d) % 32
-        mine = totals.at[y * 4 + column]
-        return remote(mine, mine, f_send.at[other], f_recv.at[y * 4 + column], {"pencil": other})
+        spot = (mask * 8 + z + d) % 16
+        mine = rounds.at[mask * 4 + column]
+        where = {"mask": spot // 8, "pencil": y * 8 + spot % 8}
+        return remote(mine, mine, f_send.at[spot], f_recv.at[mask * 4 + column], where)
 
     @pl.when(owner)
     def _():
-        each(1, 16, lambda d: told(d).wait_recv())
-        total = notes[0]
-        for spot in range(1, 16):
-            total = total + notes[spot]
-        totals[y * 4 + column] = total
-        each(1, 32, lambda d: share(d).start())
-
-    each(0, 12, lambda i: dy(1 + i // 4, i % 4, True).wait_recv())
+        each(1, 8, lambda d: tell(d, True).wait_recv())
+        rounds[mask * 4 + column] = jnp.sum(notes[...], axis=0)
+        each(1, 16, lambda d: share(d).start())
+
+    each(0, 4, dz_wait)
+    each(1, 4, lambda d: dy(d).start())
+
+    def share_wait(s):
+        theirs = rounds.at[s]
+
+        @pl.when(jnp.logical_not((s // 4 == mask) & (s % 4 == column)))
+        def _():
+            where = {"pencil": y * 8 + (z + 1) % 8}
+            remote(theirs, theirs, f_send.at[s], f_recv.at[s], where).wait_recv()
+
+    each(0, 8, share_wait)
+    totals[y] = jnp.sum(rounds[...], axis=0)
+
+    def fy(d, theirs=False):
+        other = (y + d) % 4
+        spot = other if theirs else y
+        rows = totals.at[spot]
+        return remote(rows, rows, g_send.at[other], g_recv.at[spot], {"pencil": other * 8 + z})
+
+    each(1, 4, lambda d: fy(d).start())
+
+    each(1, 4, lambda d: dy(d, True).wait_recv())
 
     band = whole[...].astype(F32).reshape(KEEP, KEEP)
     head = band[:16]
@@ -628,10 +626,10 @@
         each(1, 4, lambda d, step=step: step(d).wait_send())
     kc(0).wait_send()
     kc(1).wait_send()
-    each(0, 12, lambda i: sy(1 + i // 4, 0, i % 4).wait_send())
-    each(0, 12, lambda i: sy(1 + i // 4, 1, i % 4).wait_send())
-    each(0, 12, lambda i: cy(1 + i // 4, i % 4).wait_send())
-    each(0, 12, lambda i: dy(1 + i // 4, i % 4).wait_send())
+    each(1, 4, lambda d: sy(d, 0).wait_send())
+    each(1, 4, lambda d: sy(d, 1).wait_send())
+    each(1, 4, lambda d: cy(d).wait_send())
+    each(1, 4, lambda d: dy(d).wait_send())
 
     def sent_line(d):
         home, copy = line_to(d)
@@ -656,27 +654,17 @@
         each(1, 16, lambda d: sz(d).wait_send())
         each(1, 8, lambda d: dz(d).wait_send())
 
-    def share_wait(q):
-        theirs = totals.at[q]
-        home = q // 4 * 8 + FIRST + q % 4
-
-        @pl.when(home != pencil)
-        def _():
-            where = {"pencil": (pencil + 1) % 32}
-            remote(theirs, theirs, f_send.at[q], f_recv.at[q], where).wait_recv()
-
-    each(0, 16, share_wait)
-    total = totals[0]
-    for q in range(1, 16):
-        total = total + totals[q]
+    each(1, 4, lambda d: fy(d, True).wait_recv())
+    total = (totals[0] + totals[1]) + (totals[2] + totals[3])
     scale_out[...] = STEP_SIZE * lax.rsqrt(total[0:1] * (1.0 / 16.0) + EPSILON)
     loss_out[0, 0] = jnp.sum(jnp.where(note_row == 1, total, 0.0)) * (0.5 / (128.0 * 8.0 * N * N))
     store.wait()
+    each(1, 4, lambda d: fy(d).wait_send())
 
     @pl.when(owner)
     def _():
-        each(1, 16, lambda d: tell(d).wait_send())
-        each(1, 32, lambda d: share(d).wait_send())
+        each(1, 8, lambda d: tell(d).wait_send())
+        each(1, 16, lambda d: share(d).wait_send())
 
 
 ANY_SPEC = pl.BlockSpec(memory_space=pl.ANY)
@@ -723,17 +711,18 @@
             VMEM((8, 16, KEEP), BF16),
             VMEM((4, 4, 16, KEEP), BF16),
             VMEM((8, 128), F32),
-            VMEM((16, 8, 128), F32),
-            VMEM((16, 8, 128), F32),
+            VMEM((8, 8, 128), F32),
+            VMEM((8, 8, 128), F32),
+            VMEM((4, 8, 128), F32),
             DMA((8,)),
             DMA,
         ]
         + [DMA((8,))] * 2
         + [DMA((4,))] * 8
         + [DMA((2,))] * 2
-        + [DMA((16,)), DMA((32,)), DMA((16,)), DMA((8,)), DMA((2, 4, 4)), DMA((2, 4, 4))]
-        + [DMA((4, 4)), DMA((4, 4)), DMA((4,)), DMA((8,)), DMA((8,)), DMA((4,)), DMA((4, 4)), DMA((4, 4))]
-        + [DMA((16,)), DMA((16,)), DMA((32,)), DMA((16,))],
+        + [DMA((16,)), DMA((32,)), DMA((16,)), DMA((8,)), DMA((2, 4)), DMA((2, 4))]
+        + [DMA((4,)), DMA((4,)), DMA((4,)), DMA((8,)), DMA((8,)), DMA((4,)), DMA((4,)), DMA((4,))]
+        + [DMA((8,)), DMA((8,)), DMA((16,)), DMA((8,)), DMA((4,)), DMA((4,))],
         compiler_params=pltpu.CompilerParams(collective_id=0, has_side_effects=True, vmem_limit_bytes=LIMIT),
         name="step_kernel",
     )(

time: 85.4 us -> 80.5 us (0.943)
  Pallas kernels: 79.6 us -> 74.6 us
    pallas_call x1, Pallas kernels: 79.6 us -> 74.6 us  [per_device(): pl.pallas_call(step_kernel, out_shape=(jax.ShapeDtypeStruct((ROWS, N), BF...]
where the time goes in v3:
time: 80.5 us; the launch traced here: 80.1 us
  Pallas kernels  74.6 us (93%)
  other arithmetic  3.1 us (4%)
  between operations  2.42 us (3%)
    pallas_call x1, Pallas kernels, per_device(): pl.pallas_call(step_kernel, out_shape=(jax.ShapeDtypeStruct((ROWS, N), BF...  74.6 us
    reshape x1, other arithmetic, per_device(): return (update.reshape(1, 1, ROWS, N), loss.reshape(()))  3.1 us

profile of v3, /device:TPU:1, one launch (start us, length us, event | category | flops | bytes accessed | tf_op | source)
XLA Modules:
  0.0 80.1 jit_solution(8538169844850478514)
XLA Ops:
  0.6 0.0 copy-start
  0.6 74.6 %step_kernel.1 = (bf16[128,4096]{1,0:T(8,128)(2,1)}, f32[1,128]{1,0:T(1,128)}, f32[1,1]{1,0:T(1,128)}) custom-call(f32[128,4096]{1,0:T(8,128)} %bitcast.9, bf16[272,4096]{1,0:T(8,128)(2,1)} %constant.18.clone.ahead_hbm, bf16[4096,512]{1,0:T(8,128)(2,1)} %constant.19.clone.ahead_x_hbm, bf16[32,256,512]{2,1,0:T(8,128)(2,1)} %constant.20.clone.back_x_hbm, ...), custom_call_target="tpu_custom_call" | custom-call | tf_op jit(solution)/shard_map/step_kernel/pallas_call | solution.py:679
  75.2 0.0 copy-done
  75.3 3.1 %fusion = bf16[1,1,128,4096]{3,2,1,0:T(8,128)(2,1)} fusion(bf16[128,4096]{1,0:T(8,128)(2,1)} %get-tuple-element.6, f32[]{:T(128)} %bitcast.12, f32[1,1,128,4096]{3,2,1,0:T(8,128)S(1)} %copy-done), kind=kLoop, calls=%fused_computation.1 | loop fusion | flops 2097152 | bytes 4194308 | tf_op jit(solution)/shard_map/reshape | solution.py:734
Async XLA Ops:
  0.6 74.6 %copy-start = (f32[1,1,128,4096]{3,2,1,0:T(8,128)S(1)}, f32[1,1,128,4096]{3,2,1,0:T(8,128)}, u32[]{:S(2)}) copy-start(f32[1,1,128,4096]{3,2,1,0:T(8,128)} %param.15) | copy-start | bytes 6291460

commit v4 on v3

--- a/solution.py
+++ b/solution.py
@@ -103,18 +103,23 @@
 
 
 def each(low, high, body):
-    def step(i, carry):
+    for i in range(low, high):
         body(i)
-        return carry
-
-    lax.fori_loop(low, high, step, 0)
+
+
+def rem(value, by):
+    return value % by if isinstance(value, int) else lax.rem(value, by)
+
+
+def div(value, by):
+    return value // by if isinstance(value, int) else lax.div(value, by)
 
 
 def place():
     tile = lax.axis_index("tile")
     mask = lax.axis_index("mask")
     pencil = lax.axis_index("pencil")
-    return tile, mask, pencil, pencil // 8, pencil % 8
+    return tile, mask, pencil, div(pencil, 8), rem(pencil, 8)
 
 
 def remote(src, dst, send, recv, where):
@@ -135,7 +140,7 @@
     cy_send, cy_recv, cz_send, cz_recv, dz_send, dz_recv, dy_send, dy_recv, e_send, e_recv, f_send, f_recv, g_send, g_recv,
 ):
     tile, mask, pencil, y, z = place()
-    chip, core = (tile // 2, tile % 2)
+    chip, core = (div(tile, 2), rem(tile, 2))
     owner = (z >= FIRST) & (z < FIRST + 4)
     column = z - FIRST
     load_mask = pltpu.make_async_copy(mask_hbm, mask_ref, load_sem.at[0])
@@ -147,9 +152,9 @@
     def greet(where):
         pl.semaphore_signal(barrier, inc=1, device_id=where, device_id_type=MESH)
 
-    each(1, 32, lambda d: greet({"pencil": (pencil + d) % 32}))
+    each(1, 32, lambda d: greet({"pencil": rem(pencil + d, 32)}))
     each(0, 8, lambda d: greet({"mask": 1 - mask, "pencil": y * 8 + d}))
-    each(1, 8, lambda d: greet({"tile": (tile + d) % 8}))
+    each(1, 8, lambda d: greet({"tile": rem(tile + d, 8)}))
 
     sub = iota((8, KEEP), 0)
     lane = iota((8, KEEP), 1)
@@ -221,16 +226,16 @@
         return remote(rows, rows, send.at[other], recv.at[spot], where)
 
     def kz(d, theirs=False):
-        other = (z + d) % 8
+        other = rem(z + d, 8)
         spot = other if theirs else z
         return hop(kern.at[core, chip, y, spot], kz_send, kz_recv, other, spot, {"pencil": y * 8 + other})
 
     def along_x(d, theirs):
-        other = (chip + d) % 4
+        other = rem(chip + d, 4)
         return other, other if theirs else chip, {"tile": other * 2 + core}
 
     def along_y(d, theirs):
-        other = (y + d) % 4
+        other = rem(y + d, 4)
         return other, other if theirs else y, {"pencil": other * 8 + z}
 
     def ka(d, theirs=False):
@@ -259,10 +264,10 @@
     own_lines = lines_ref.at[:, pl.ds(pl.multiple_of(pencil * ROWS, ROWS), ROWS)]
 
     def line_to(d):
-        q = (pencil // 2 + d) % 16
-        home = q // 4 * 8 + FIRST + q % 4
+        q = rem(div(pencil, 2) + d, 16)
+        home = div(q, 4) * 8 + FIRST + rem(q, 4)
         src = line_ref.at[pl.ds(pl.multiple_of(q * 16, 16), 16)]
-        return home, remote(src, own_lines, a_send.at[q], a_recv.at[pencil], {"pencil": home})
+        return home, remote(src, own_lines, a_send.at[q], a_recv, {"pencil": home})
 
     def send_line(d):
         home, copy = line_to(d)
@@ -294,22 +299,18 @@
     each(1, 4, lambda d: ke(d).start())
 
     def sz(d):
-        spot = (mask * 8 + z + d) % 16
+        side = mask if d < 8 else 1 - mask
+        other = rem(z + d, 8)
         mine = seen.at[y, mask, column]
-        where = {"mask": spot // 8, "pencil": y * 8 + spot % 8}
-        return remote(mine, mine, sz_send.at[spot], sz_recv.at[mask * 4 + column], where)
+        where = {"mask": side, "pencil": y * 8 + other}
+        return remote(mine, mine, sz_send.at[side * 8 + other], sz_recv.at[mask * 4 + column], where)
 
     later[0].wait()
 
     @pl.when(owner)
     def _():
-        def line_from(d):
-            other = (pencil + d) % 32
-            src = line_ref.at[pl.ds(0, 16)]
-            dst = lines_ref.at[:, pl.ds(pl.multiple_of(other * ROWS, ROWS), ROWS)]
-            return remote(src, dst, a_send.at[0], a_recv.at[other], {"pencil": other})
-
-        each(1, 32, lambda d: line_from(d).wait_recv())
+        others = lines_ref.at[:, pl.ds(0, 31 * ROWS)]
+        remote(others, others, a_send.at[0], a_recv, {"pencil": rem(pencil + 1, 32)}).wait_recv()
         held = lines_ref[...].astype(F32)
         first = (y == 0) & (column == 0)
         stash = (iota((16, N), 0) == 8) & first
@@ -344,11 +345,11 @@
 
         @pl.when(jnp.logical_not(mine))
         def _():
-            where = {"pencil": y * 8 + (z + 1) % 8}
+            where = {"pencil": y * 8 + rem(z + 1, 8)}
             remote(theirs, theirs, sz_send.at[q], sz_recv.at[m * 4 + q], where).wait_recv()
 
     def sy(d, m, theirs=False):
-        other = (y + d) % 4
+        other = rem(y + d, 4)
         spot = other if theirs else y
         rows = seen.at[spot, m]
         return remote(rows, rows, sy_send.at[m, other], sy_recv.at[m, spot], {"pencil": other * 8 + z})
@@ -490,7 +491,7 @@
     part_ref[...] = dot_nn(merge_ref[...], full).astype(BF16).reshape(4, 4, 16, KEEP)
 
     def cy(d, theirs=False):
-        other = (y + d) % 4
+        other = rem(y + d, 4)
         spot = other if theirs else y
         where = {"pencil": other * 8 + z}
         return remote(part_ref.at[other], gathered.at[spot], cy_send.at[other], cy_recv.at[spot], where)
@@ -516,7 +517,7 @@
     each(0, 4, send_piece)
 
     def dz(d):
-        other = (z + d) % 8
+        other = rem(z + d, 8)
         mine = whole.at[y, column]
         return remote(mine, mine, dz_send.at[other], dz_recv.at[column], {"pencil": y * 8 + other})
 
@@ -525,7 +526,7 @@
     note_row = iota((8, 128), 0)
 
     def tell(d, theirs=False):
-        other = (tile + d) % 8
+        other = rem(tile + d, 8)
         spot = other if theirs else tile
         return remote(note, notes.at[spot], e_send.at[other], e_recv.at[spot], {"tile": other})
 
@@ -534,7 +535,7 @@
         pieces[z] = summed[column]
 
         def piece_from(d):
-            other = (z + d) % 8
+            other = rem(z + d, 8)
             where = {"pencil": y * 8 + other}
             return remote(summed.at[0], pieces.at[other], cz_send.at[0], cz_recv.at[other], where)
 
@@ -558,19 +559,20 @@
 
         @pl.when(q != column)
         def _():
-            where = {"pencil": y * 8 + (z + 1) % 8}
+            where = {"pencil": y * 8 + rem(z + 1, 8)}
             remote(theirs, theirs, dz_send.at[q], dz_recv.at[q], where).wait_recv()
 
     def dy(d, theirs=False):
-        other = (y + d) % 4
+        other = rem(y + d, 4)
         spot = other if theirs else y
         rows = whole.at[spot]
         return remote(rows, rows, dy_send.at[other], dy_recv.at[spot], {"pencil": other * 8 + z})
 
-    def share(d):
-        spot = (mask * 8 + z + d) % 16
+    def share(step):
+        d = 8 + div(step, 2) * (1 if step % 2 else -1)
+        spot = rem(mask * 8 + z + d, 16)
         mine = rounds.at[mask * 4 + column]
-        where = {"mask": spot // 8, "pencil": y * 8 + spot % 8}
+        where = {"mask": div(spot, 8), "pencil": y * 8 + rem(spot, 8)}
         return remote(mine, mine, f_send.at[spot], f_recv.at[mask * 4 + column], where)
 
     @pl.when(owner)
@@ -587,14 +589,14 @@
 
         @pl.when(jnp.logical_not((s // 4 == mask) & (s % 4 == column)))
         def _():
-            where = {"pencil": y * 8 + (z + 1) % 8}
+            where = {"pencil": y * 8 + rem(z + 1, 8)}
             remote(theirs, theirs, f_send.at[s], f_recv.at[s], where).wait_recv()
 
     each(0, 8, share_wait)
     totals[y] = jnp.sum(rounds[...], axis=0)
 
     def fy(d, theirs=False):
-        other = (y + d) % 4
+        other = rem(y + d, 4)
         spot = other if theirs else y
         rows = totals.at[spot]
         return remote(rows, rows, g_send.at[other], g_recv.at[spot], {"pencil": other * 8 + z})
@@ -720,7 +722,7 @@
         + [DMA((8,))] * 2
         + [DMA((4,))] * 8
         + [DMA((2,))] * 2
-        + [DMA((16,)), DMA((32,)), DMA((16,)), DMA((8,)), DMA((2, 4)), DMA((2, 4))]
+        + [DMA((16,)), DMA, DMA((16,)), DMA((8,)), DMA((2, 4)), DMA((2, 4))]
         + [DMA((4,)), DMA((4,)), DMA((4,)), DMA((8,)), DMA((8,)), DMA((4,)), DMA((4,)), DMA((4,))]
         + [DMA((8,)), DMA((8,)), DMA((16,)), DMA((8,)), DMA((4,)), DMA((4,))],
         compiler_params=pltpu.CompilerParams(collective_id=0, has_side_effects=True, vmem_limit_bytes=LIMIT),

time: 80.5 us -> 79.6 us (0.989)
  no operation moved by 1% of the time
where the time goes in v4:
time: 79.6 us; the launch traced here: 79.4 us
  Pallas kernels  73.9 us (93%)
  other arithmetic  3.1 us (4%)
  between operations  2.42 us (3%)
    pallas_call x1, Pallas kernels, per_device(): pl.pallas_call(step_kernel, out_shape=(jax.ShapeDtypeStruct((ROWS, N), BF...  73.9 us
    reshape x1, other arithmetic, per_device(): return (update.reshape(1, 1, ROWS, N), loss.reshape(()))  3.1 us

profile of v4, /device:TPU:1, one launch (start us, length us, event | category | flops | bytes accessed | tf_op | source)
XLA Modules:
  0.0 79.4 jit_solution(592920017927161782)
XLA Ops:
  0.6 0.0 copy-start
  0.6 73.9 %step_kernel.1 = (bf16[128,4096]{1,0:T(8,128)(2,1)}, f32[1,128]{1,0:T(1,128)}, f32[1,1]{1,0:T(1,128)}) custom-call(f32[128,4096]{1,0:T(8,128)} %bitcast.9, bf16[272,4096]{1,0:T(8,128)(2,1)} %constant.18.clone.ahead_hbm, bf16[4096,512]{1,0:T(8,128)(2,1)} %constant.19.clone.ahead_x_hbm, bf16[32,256,512]{2,1,0:T(8,128)(2,1)} %constant.20.clone.back_x_hbm, ...), custom_call_target="tpu_custom_call" | custom-call | tf_op jit(solution)/shard_map/step_kernel/pallas_call | solution.py:681
  74.5 0.0 copy-done
  74.6 3.1 %fusion = bf16[1,1,128,4096]{3,2,1,0:T(8,128)(2,1)} fusion(bf16[128,4096]{1,0:T(8,128)(2,1)} %get-tuple-element.6, f32[]{:T(128)} %bitcast.12, f32[1,1,128,4096]{3,2,1,0:T(8,128)S(1)} %copy-done), kind=kLoop, calls=%fused_computation.1 | loop fusion | flops 2097152 | bytes 4194308 | tf_op jit(solution)/shard_map/reshape | solution.py:736
Async XLA Ops:
  0.6 73.9 %copy-start = (f32[1,1,128,4096]{3,2,1,0:T(8,128)S(1)}, f32[1,1,128,4096]{3,2,1,0:T(8,128)}, u32[]{:S(2)}) copy-start(f32[1,1,128,4096]{3,2,1,0:T(8,128)} %param.15) | copy-start | bytes 6291460

commit v5 on v4

--- a/solution.py
+++ b/solution.py
@@ -429,7 +429,7 @@
     image = jnp.concatenate(images, axis=0).astype(BF16)
 
     loss = jnp.zeros((ROWS, 128), F32)
-    picked = jnp.zeros((2 * ROWS, 3 * PTS), F32)
+    picked = jnp.zeros((ROWS, 3 * PTS), F32)
     for base in range(0, N, CHUNK):
         at = slice(base, base + CHUNK)
         fine = dot_nn(image, spread[:, at])
@@ -440,12 +440,10 @@
         slope_ref[:, at] = 12.0 * product * (1.0 - own)
         gap = union - target[:, at].astype(F32)
         gap_ref[:, at] = gap
-        high = union.astype(BF16)
-        rest = (union - high.astype(F32)).astype(BF16)
-        picked = picked + dot_nn(jnp.concatenate([high, rest], axis=0), hot_t_ref[at, :])
+        picked = picked + dot_nn(union.astype(BF16), hot_t_ref[at, :])
         square = gap * gap
         loss = loss + (square[:, :128] + square[:, 128:256]) + (square[:, 256:384] + square[:, 384:])
-    missed = jnp.sum((picked[:ROWS] + picked[ROWS:]) * row_hot, axis=0, keepdims=True) - goal
+    missed = jnp.sum(picked * row_hot, axis=0, keepdims=True) - goal
     push = weight * missed
     loss = jnp.sum(loss) + jnp.sum(push * missed)
     hits = (row_hot * push).astype(BF16)
@@ -454,20 +452,22 @@
         at = slice(base, base + CHUNK)
         pull = gap_ref[:, at] + dot_nn(hits, hot_ref[:, at])
         drive = drive + dot_nn((pull * slope_ref[:, at]).astype(BF16), spread_t[at, :])
-    drive = jnp.concatenate([drive, drive], axis=1)
-    drive = jnp.concatenate([drive] * KERN, axis=0)
-    mixed = (drive * fields[...].astype(F32)).astype(BF16)
-    lines = dot_nt(back_y[...], mixed)
     sum_real = jnp.zeros((KEEP, KEEP), F32)
     sum_imag = jnp.zeros((KEEP, KEEP), F32)
-    for k in range(KERN):
-        at = slice(k * ROWS, (k + 1) * ROWS)
-        line = jnp.concatenate([lines[:KEEP, at], lines[KEEP:, at]], axis=1).astype(BF16)
-        back = dot_nn(line, back_x[...])
-        back_real, back_imag = (back[:, :KEEP], back[:, KEEP:])
-        kern_real, kern_imag = (bands[k], bands[KERN + k])
-        sum_real = sum_real + (kern_real * back_real + kern_imag * back_imag)
-        sum_imag = sum_imag + (kern_real * back_imag - kern_imag * back_real)
+    wide_drive = jnp.concatenate([drive, drive], axis=1)
+    for pair in range(0, KERN, 2):
+        mixed = [
+            (wide_drive * fields[k * ROWS : k * ROWS + ROWS].astype(F32)).astype(BF16) for k in (pair, pair + 1)
+        ]
+        lines = dot_nt(back_y[...], jnp.concatenate(mixed, axis=0))
+        for k in (pair, pair + 1):
+            at = slice((k - pair) * ROWS, (k - pair + 1) * ROWS)
+            line = jnp.concatenate([lines[:KEEP, at], lines[KEEP:, at]], axis=1).astype(BF16)
+            back = dot_nn(line, back_x[...])
+            back_real, back_imag = (back[:, :KEEP], back[:, KEEP:])
+            kern_real, kern_imag = (bands[k], bands[KERN + k])
+            sum_real = sum_real + (kern_real * back_real + kern_imag * back_imag)
+            sum_imag = sum_imag + (kern_real * back_imag - kern_imag * back_real)
     sum_real = sum_real * (2.0 / (N * N))
     sum_imag = sum_imag * (2.0 / (N * N))
 

time: 79.6 us -> 79.7 us (level)
  no operation moved by 1% of the time
where the time goes in v5:
time: 79.7 us; the launch traced here: 79.5 us
  Pallas kernels  74 us (93%)
  other arithmetic  3.1 us (4%)
  between operations  2.42 us (3%)
    pallas_call x1, Pallas kernels, per_device(): pl.pallas_call(step_kernel, out_shape=(jax.ShapeDtypeStruct((ROWS, N), BF...  74 us
    reshape x1, other arithmetic, per_device(): return (update.reshape(1, 1, ROWS, N), loss.reshape(()))  3.1 us

profile of v5, /device:TPU:1, one launch (start us, length us, event | category | flops | bytes accessed | tf_op | source)
XLA Modules:
  0.0 79.5 jit_solution(16602371464927539943)
XLA Ops:
  0.6 0.0 copy-start
  0.6 74.0 %step_kernel.1 = (bf16[128,4096]{1,0:T(8,128)(2,1)}, f32[1,128]{1,0:T(1,128)}, f32[1,1]{1,0:T(1,128)}) custom-call(f32[128,4096]{1,0:T(8,128)} %bitcast.9, bf16[272,4096]{1,0:T(8,128)(2,1)} %constant.18.clone.ahead_hbm, bf16[4096,512]{1,0:T(8,128)(2,1)} %constant.19.clone.ahead_x_hbm, bf16[32,256,512]{2,1,0:T(8,128)(2,1)} %constant.20.clone.back_x_hbm, ...), custom_call_target="tpu_custom_call" | custom-call | tf_op jit(solution)/shard_map/step_kernel/pallas_call | solution.py:681
  74.6 0.0 copy-done
  74.7 3.1 %fusion = bf16[1,1,128,4096]{3,2,1,0:T(8,128)(2,1)} fusion(bf16[128,4096]{1,0:T(8,128)(2,1)} %get-tuple-element.6, f32[]{:T(128)} %bitcast.12, f32[1,1,128,4096]{3,2,1,0:T(8,128)S(1)} %copy-done), kind=kLoop, calls=%fused_computation.1 | loop fusion | flops 2097152 | bytes 4194308 | tf_op jit(solution)/shard_map/reshape | solution.py:736
Async XLA Ops:
  0.6 74.0 %copy-start = (f32[1,1,128,4096]{3,2,1,0:T(8,128)S(1)}, f32[1,1,128,4096]{3,2,1,0:T(8,128)}, u32[]{:S(2)}) copy-start(f32[1,1,128,4096]{3,2,1,0:T(8,128)} %param.15) | copy-start | bytes 6291460
